TPU v7x, 32 devices: a whole 2x2x4 slice. The times are simulated.
32 devices in a mesh: dp: 2 (over x), context: 4 (over z), expert: 4 (over y, core).
Axes of the slice: x: 2, y: 2, z: 4, core: 2. Of those that a mesh axis runs over, the one named last changes fastest.
Arguments:
- packed_in: bfloat16 [8, 1024, 1536], P(('dp', 'expert'), 'context'), may hold values from -6 to 6
- routes: int32 [8, 1024, 4], P(('dp', 'expert'), 'context'), may hold values from 0 to 7, all different within a row; in each aligned block of 256 rows (0 to 255, 256 to 511, ..., all dimensions but the last counted through in order) at most 192 rows name the same one
- gates: float32 [8, 1024, 4], P(('dp', 'expert'), 'context'), may hold values from 0.1 to 0.4
- doc_starts: int32 [8, 6], P(('dp', 'expert')), may hold values from 0 to 1023, as said below
- attn_gain: float32 [1536], replicated, may hold values from 0.5 to 1.5
- w_qkv: bfloat16 [1536, 2048], replicated, may hold values from -0.15625 to 0.15625
- w_out: bfloat16 [1536, 1536], replicated, may hold values from -2.5 to 2.5
- ffn_gain: float32 [1536], replicated, may hold values from 0.5 to 1.5
- expert_gate_up: bfloat16 [8, 1536, 1536], P('expert'), may hold values from -0.15625 to 0.15625
- expert_down: bfloat16 [8, 768, 1536], P('expert'), may hold values from -0.875 to 0.875
- cotangent: bfloat16 [8, 1024, 1536], P(('dp', 'expert'), 'context'), may hold values from -6 to 6
Outputs:
- packed_out: bfloat16 [8, 1024, 1536], P(('dp', 'expert'), 'context')
- packed_grad: float32 [8, 1024, 1536], P(('dp', 'expert'), 'context')
- attn_gain_grad: float32 [1536], P('context')
- qkv_grad: float32 [1536, 2048], P('context')
- out_proj_grad: float32 [1536, 1536], P('context')
- ffn_gain_grad: float32 [1536], P('context')
- gate_up_grad: float32 [8, 1536, 1536], P('expert', 'context')
- down_grad: float32 [8, 768, 1536], P('expert', 'context')
Inputs may be any that keep to these rules, and one draw needn't show every extreme that they name: `routes`: each token names 4 different experts; among the 256 tokens of one device (aligned blocks along a pack) no expert is named more than 192 times. `doc_starts`: each row holds the first positions of the 6 documents of one pack, strictly increasing, the first 0; a document runs to the next start or to the pack's end.
All inputs are finite; a program needn't handle non-finite values.
Results may differ from a plain program's by a relative error of at most 0.025.
Values may be sent and summed in bfloat16 or wider, within the bound.
A program may use at most 192 MiB of HBM per device.

v0:
```python
import jax
import jax.numpy as jnp
from jax import lax
from jax.sharding import PartitionSpec as P

D = 1536
QUERY_HEADS = 12
KEY_VALUE_HEADS = 2
HEAD_SIZE = 128
FF = 768
TOP = 4
CAP = 192


epsilon = 1e-06
rope_base = 10000.0
negative_huge = -1e30


def smooth_gate(preact):
    return jax.nn.gelu(preact, approximate=True)


def norm_rows(values, gain):
    inverse = lax.rsqrt(jnp.mean(values * values, axis=-1, keepdims=True) + epsilon)
    return (values * inverse * gain, inverse)


def norm_back(values, inverse, gain, upstream):
    scaled = upstream * gain
    inner = jnp.mean(scaled * values, axis=-1, keepdims=True)
    grad_in = inverse * scaled - values * inverse * inverse * inverse * inner
    grad_gain = jnp.sum(upstream * values * inverse, axis=0)
    return (grad_in, grad_gain)


def doc_begins(positions, starts):
    return jnp.max(jnp.where(starts[None, :] <= positions[:, None], starts[None, :], 0), axis=1)


def rope_tables(offsets, half_dim):
    frequency = rope_base ** (-(jnp.arange(half_dim, dtype=jnp.float32) * 2.0 / (2.0 * half_dim)))
    angles = offsets.astype(jnp.float32)[:, None] * frequency[None, :]
    return (jnp.cos(angles), jnp.sin(angles))


def apply_rotary(values, cosine_table, sine_values, forward):
    half_dim = cosine_table.shape[1]
    first = values[..., :half_dim]
    second = values[..., half_dim:]
    cosine_wide = cosine_table[:, None, :]
    sine_wide = sine_values[:, None, :]
    if forward:
        return jnp.concatenate(
            [first * cosine_wide - second * sine_wide, second * cosine_wide + first * sine_wide],
            axis=-1,
        )
    return jnp.concatenate(
        [first * cosine_wide + second * sine_wide, second * cosine_wide - first * sine_wide],
        axis=-1,
    )


def fold_keys(
    folded, key_matrix, value_matrix, key_start, query_matrix, positions, begins, scaling
):
    running_max, denominator, weighted = folded
    row_count = key_matrix.shape[0]
    key_pos = key_start + jnp.arange(row_count, dtype=jnp.int32)
    allowed = (key_pos[None, :] <= positions[:, None]) & (key_pos[None, :] >= begins[:, None])
    scores = (
        jnp.einsum("qgha,kga->ghqk", query_matrix, key_matrix, preferred_element_type=jnp.float32)
        * scaling
    )
    masked = jnp.where(allowed, scores, negative_huge)
    new_max = jnp.maximum(running_max, jnp.max(masked, axis=-1))
    weights = jnp.where(allowed, jnp.exp(scores - new_max[..., None]), 0.0)
    shrink = jnp.exp(running_max - new_max)
    denominator = denominator * shrink + jnp.sum(weights, axis=-1)
    weighted = weighted * shrink[..., None] + jnp.einsum(
        "ghqk,kga->ghqa",
        weights.astype(jnp.bfloat16),
        value_matrix,
        preferred_element_type=jnp.float32,
    )
    return (new_max, denominator, weighted)


def attend_back(
    query_matrix,
    output_gradient,
    logsum,
    delta,
    positions,
    begins,
    key_matrix,
    value_matrix,
    key_start,
    scaling,
):
    row_count = key_matrix.shape[0]
    key_pos = key_start + jnp.arange(row_count, dtype=jnp.int32)
    allowed = (key_pos[None, :] <= positions[:, None]) & (key_pos[None, :] >= begins[:, None])
    scores = (
        jnp.einsum("qgha,kga->ghqk", query_matrix, key_matrix, preferred_element_type=jnp.float32)
        * scaling
    )
    probs = jnp.where(allowed, jnp.exp(scores - logsum[..., None]), 0.0)
    grad_probs = jnp.einsum(
        "ghqa,kga->ghqk", output_gradient, value_matrix, preferred_element_type=jnp.float32
    )
    grad_scores = (probs * (grad_probs - delta[..., None])).astype(jnp.bfloat16)
    grad_query = (
        jnp.einsum("ghqk,kga->ghqa", grad_scores, key_matrix, preferred_element_type=jnp.float32)
        * scaling
    )
    grad_key = (
        jnp.einsum("ghqk,qgha->kga", grad_scores, query_matrix, preferred_element_type=jnp.float32)
        * scaling
    )
    grad_value = jnp.einsum(
        "ghqk,ghqa->kga",
        probs.astype(jnp.bfloat16),
        output_gradient,
        preferred_element_type=jnp.float32,
    )
    return (grad_query, grad_key, grad_value)


def body(
    packed_in,
    routes,
    gates,
    doc_starts,
    attn_gain,
    w_qkv,
    w_out,
    ffn_gain,
    expert_gate_up,
    expert_down,
    cotangent,
):
    tokens = packed_in[0].astype(jnp.float32)
    token_count = tokens.shape[0]
    query_groups = QUERY_HEADS // KEY_VALUE_HEADS
    query_width = QUERY_HEADS * HEAD_SIZE
    key_value_width = KEY_VALUE_HEADS * HEAD_SIZE
    scaling = HEAD_SIZE ** (-0.5)
    contexts = lax.axis_size("context")
    own_index = lax.axis_index("context")
    positions = own_index * token_count + jnp.arange(token_count, dtype=jnp.int32)
    last_pos = own_index * token_count + token_count - 1
    begins = doc_begins(positions, doc_starts[0])
    cosine_table, sine_values = rope_tables(positions - begins, HEAD_SIZE // 2)
    normed_a, inverse_a = norm_rows(tokens, attn_gain)
    normed_ab = normed_a.astype(jnp.bfloat16)
    projected_rows = jnp.dot(normed_ab, w_qkv, preferred_element_type=jnp.float32)
    query_matrix = apply_rotary(
        projected_rows[:, :query_width].reshape(token_count, QUERY_HEADS, HEAD_SIZE),
        cosine_table,
        sine_values,
        True,
    )
    query_matrix = query_matrix.astype(jnp.bfloat16).reshape(
        token_count, KEY_VALUE_HEADS, query_groups, HEAD_SIZE
    )
    key_matrix = apply_rotary(
        projected_rows[:, query_width : query_width + key_value_width].reshape(
            token_count, KEY_VALUE_HEADS, HEAD_SIZE
        ),
        cosine_table,
        sine_values,
        True,
    )
    key_matrix = key_matrix.astype(jnp.bfloat16)
    value_matrix = (
        projected_rows[:, query_width + key_value_width :]
        .reshape(token_count, KEY_VALUE_HEADS, HEAD_SIZE)
        .astype(jnp.bfloat16)
    )
    query_layout = (KEY_VALUE_HEADS, query_groups, token_count, HEAD_SIZE)
    start_state = (
        jnp.full((KEY_VALUE_HEADS, query_groups, token_count), negative_huge, jnp.float32),
        jnp.zeros((KEY_VALUE_HEADS, query_groups, token_count), jnp.float32),
        jnp.zeros(query_layout, jnp.float32),
    )
    part_keys = lax.all_gather(key_matrix, "context", axis=0, tiled=True)
    part_values = lax.all_gather(value_matrix, "context", axis=0, tiled=True)
    row_count = part_keys.shape[0]
    width = 512 if row_count > 1024 and row_count % 512 == 0 else row_count

    def inner_step(block_index, state_now):
        offset = block_index * width
        block_keys = lax.dynamic_slice_in_dim(part_keys, block_index * width, width, 0)
        block_values = lax.dynamic_slice_in_dim(part_values, block_index * width, width, 0)

        def update(state_in):
            return fold_keys(
                state_in, block_keys, block_values, offset, query_matrix, positions, begins, scaling
            )

        def unchanged(state_in):
            return state_in

        return lax.cond(offset <= last_pos, update, unchanged, state_now)

    running_max, denominator, weighted = lax.fori_loop(
        0, row_count // width, inner_step, start_state
    )
    attended = weighted / denominator[..., None]
    logsum = running_max + jnp.log(denominator)
    merged_b = (
        jnp.transpose(attended, (2, 0, 1, 3)).reshape(token_count, query_width).astype(jnp.bfloat16)
    )
    residual = tokens + jnp.dot(merged_b, w_out, preferred_element_type=jnp.float32)
    normed_f, inverse_f = norm_rows(residual, ffn_gain)
    normed_fb = normed_f.astype(jnp.bfloat16)
    local_experts = expert_gate_up.shape[0]
    expert_devices = lax.axis_size("expert")
    expert_total = local_experts * expert_devices
    chosen = routes[0].reshape(-1)
    onehot = (chosen[:, None] == jnp.arange(expert_total, dtype=jnp.int32)[None, :]).astype(
        jnp.int32
    )
    slots = jnp.sum((jnp.cumsum(onehot, axis=0) - onehot) * onehot, axis=1)
    repeated = jnp.repeat(normed_fb, TOP, axis=0)
    outgoing = jnp.zeros((expert_total, CAP, D), jnp.bfloat16).at[chosen, slots].set(repeated)
    outgoing = outgoing.reshape(expert_devices, local_experts, CAP, D)
    arrived_rows = lax.all_to_all(outgoing, "expert", split_axis=0, concat_axis=0, tiled=True)
    gate_up_rows = jnp.einsum(
        "sjcd,jdf->sjcf", arrived_rows, expert_gate_up, preferred_element_type=jnp.float32
    )
    hidden = (smooth_gate(gate_up_rows[..., :FF]) * gate_up_rows[..., FF:]).astype(jnp.bfloat16)
    produced = jnp.einsum("sjcf,jfd->sjcd", hidden, expert_down, preferred_element_type=jnp.float32)
    returned_rows = lax.all_to_all(
        produced.astype(jnp.bfloat16), "expert", split_axis=0, concat_axis=0, tiled=True
    )
    picked = (
        returned_rows.reshape(expert_total, CAP, D)[chosen, slots]
        .astype(jnp.float32)
        .reshape(token_count, TOP, D)
    )
    gate_values = gates[0]
    mixture = jnp.sum(gate_values[..., None] * picked, axis=1)
    packed_out = (residual + mixture).astype(jnp.bfloat16)
    upstream = cotangent[0].astype(jnp.float32)
    grad_mix = (
        (gate_values[..., None] * upstream[:, None, :])
        .astype(jnp.bfloat16)
        .reshape(token_count * TOP, D)
    )
    grad_send = jnp.zeros((expert_total, CAP, D), jnp.bfloat16).at[chosen, slots].set(grad_mix)
    grad_send = grad_send.reshape(expert_devices, local_experts, CAP, D)
    grad_arrived = lax.all_to_all(grad_send, "expert", split_axis=0, concat_axis=0, tiled=True)
    gate_part = gate_up_rows[..., :FF]
    up_part = gate_up_rows[..., FF:]
    activated, gelu_back = jax.vjp(smooth_gate, gate_part)
    hidden_b = (activated * up_part).astype(jnp.bfloat16)
    grad_hidden = jnp.einsum(
        "sjcd,jfd->sjcf", grad_arrived, expert_down, preferred_element_type=jnp.float32
    )
    down_grad = jnp.einsum(
        "sjcf,sjcd->jfd", hidden_b, grad_arrived, preferred_element_type=jnp.float32
    )
    grad_gate = gelu_back(grad_hidden * up_part)[0]
    grad_gu = jnp.concatenate([grad_gate, grad_hidden * activated], axis=-1).astype(jnp.bfloat16)
    gate_up_grad = jnp.einsum(
        "sjcd,sjcf->jdf", arrived_rows, grad_gu, preferred_element_type=jnp.float32
    )
    grad_rows = jnp.einsum(
        "sjcf,jdf->sjcd", grad_gu, expert_gate_up, preferred_element_type=jnp.float32
    )
    grad_back = lax.all_to_all(
        grad_rows.astype(jnp.bfloat16), "expert", split_axis=0, concat_axis=0, tiled=True
    )
    grad_picked = grad_back.reshape(expert_total, CAP, D)[chosen, slots].astype(jnp.float32)
    grad_normed_f = jnp.sum(grad_picked.reshape(token_count, TOP, D), axis=1)
    grad_resid_part, ffn_gain_grad = norm_back(residual, inverse_f, ffn_gain, grad_normed_f)
    grad_residual = upstream + grad_resid_part
    grad_branch = grad_residual.astype(jnp.bfloat16)
    out_proj_grad = jnp.einsum(
        "td,tf->df", merged_b, grad_branch, preferred_element_type=jnp.float32
    )
    merged_gradient = jnp.einsum(
        "tf,df->td", grad_branch, w_out, preferred_element_type=jnp.float32
    ).astype(jnp.bfloat16)
    output_gradient = jnp.transpose(
        merged_gradient.reshape(token_count, KEY_VALUE_HEADS, query_groups, HEAD_SIZE), (1, 2, 0, 3)
    )
    delta = jnp.sum(output_gradient.astype(jnp.float32) * attended, axis=-1)

    def block_back(part_keys, part_values, key_start):

        def compute(operands):
            return attend_back(
                query_matrix,
                output_gradient,
                logsum,
                delta,
                positions,
                begins,
                operands[0],
                operands[1],
                key_start,
                scaling,
            )

        def nothing(operands):
            return (
                jnp.zeros(query_layout, jnp.float32),
                jnp.zeros(operands[0].shape, jnp.float32),
                jnp.zeros(operands[1].shape, jnp.float32),
            )

        return lax.cond(key_start <= last_pos, compute, nothing, (part_keys, part_values))

    grad_query = jnp.zeros(query_layout, jnp.float32)
    complete_keys, whole_values = (
        lax.all_gather(key_matrix, "context", axis=0, tiled=True),
        lax.all_gather(value_matrix, "context", axis=0, tiled=True),
    )
    block_span = 2 * token_count

    def block_turn(turn_index, block_state):
        keys_grad_all, values_grad_all, query_sum = block_state
        offset = turn_index * block_span
        add_query, add_key, add_value = block_back(
            lax.dynamic_slice_in_dim(complete_keys, offset, block_span, 0),
            lax.dynamic_slice_in_dim(whole_values, offset, block_span, 0),
            offset,
        )
        keys_grad_all = lax.dynamic_update_slice_in_dim(keys_grad_all, add_key, offset, 0)
        values_grad_all = lax.dynamic_update_slice_in_dim(values_grad_all, add_value, offset, 0)
        return (keys_grad_all, values_grad_all, query_sum + add_query)

    zero_filled = jnp.zeros((complete_keys.shape[0], KEY_VALUE_HEADS, HEAD_SIZE), jnp.float32)
    finished = lax.fori_loop(0, contexts // 2, block_turn, (zero_filled, zero_filled, grad_query))
    grad_keys, grad_values = (
        lax.psum_scatter(
            finished[0].astype(jnp.bfloat16), "context", scatter_dimension=0, tiled=True
        ).astype(jnp.float32),
        lax.psum_scatter(
            finished[1].astype(jnp.bfloat16), "context", scatter_dimension=0, tiled=True
        ).astype(jnp.float32),
    )
    grad_query = finished[2]
    grad_q_rows = apply_rotary(
        jnp.transpose(grad_query, (2, 0, 1, 3)).reshape(token_count, QUERY_HEADS, HEAD_SIZE),
        cosine_table,
        sine_values,
        False,
    )
    grad_k_rows = apply_rotary(grad_keys, cosine_table, sine_values, False)
    grad_projected = jnp.concatenate(
        [
            grad_q_rows.reshape(token_count, query_width),
            grad_k_rows.reshape(token_count, key_value_width),
            grad_values.reshape(token_count, key_value_width),
        ],
        axis=-1,
    ).astype(jnp.bfloat16)
    qkv_grad = jnp.einsum(
        "td,tf->df", normed_ab, grad_projected, preferred_element_type=jnp.float32
    )
    grad_normed_a = jnp.einsum(
        "tf,df->td", grad_projected, w_qkv, preferred_element_type=jnp.float32
    )
    grad_in_part, attn_gain_grad = norm_back(tokens, inverse_a, attn_gain, grad_normed_a)
    packed_grad = grad_residual + grad_in_part
    summed = (
        lax.psum_scatter(
            attn_gain_grad.astype(jnp.bfloat16), "context", scatter_dimension=0, tiled=True
        ).astype(jnp.float32),
        lax.psum_scatter(
            qkv_grad.astype(jnp.bfloat16), "context", scatter_dimension=0, tiled=True
        ).astype(jnp.float32),
        lax.psum_scatter(
            out_proj_grad.astype(jnp.bfloat16), "context", scatter_dimension=0, tiled=True
        ).astype(jnp.float32),
        lax.psum_scatter(
            ffn_gain_grad.astype(jnp.bfloat16), "context", scatter_dimension=0, tiled=True
        ).astype(jnp.float32),
        lax.psum_scatter(
            gate_up_grad.astype(jnp.bfloat16), "context", scatter_dimension=1, tiled=True
        ).astype(jnp.float32),
        lax.psum_scatter(
            down_grad.astype(jnp.bfloat16), "context", scatter_dimension=1, tiled=True
        ).astype(jnp.float32),
    )
    dense_rows = (summed[0], summed[1], summed[2], summed[3])
    expert_sums = (
        lax.psum(summed[4].astype(jnp.bfloat16), "dp").astype(jnp.float32),
        lax.psum(summed[5].astype(jnp.bfloat16), "dp").astype(jnp.float32),
    )
    shared = (
        lax.psum(dense_rows[0].astype(jnp.bfloat16), ("dp", "expert")).astype(jnp.float32),
        lax.psum(dense_rows[1].astype(jnp.bfloat16), ("dp", "expert")).astype(jnp.float32),
        lax.psum(dense_rows[2].astype(jnp.bfloat16), ("dp", "expert")).astype(jnp.float32),
        lax.psum(dense_rows[3].astype(jnp.bfloat16), ("dp", "expert")).astype(jnp.float32),
    )
    return (
        packed_out[None],
        packed_grad[None],
        shared[0],
        shared[1],
        shared[2],
        shared[3],
        expert_sums[0],
        expert_sums[1],
    )


def solution(mesh):
    placed = (
        P(("dp", "expert"), "context", None),
        P(("dp", "expert"), "context", None),
        P(("dp", "expert"), "context", None),
        P(("dp", "expert"), None),
        P(),
        P(),
        P(),
        P(),
        P("expert", None, None),
        P("expert", None, None),
        P(("dp", "expert"), "context", None),
    )
    return jax.shard_map(
        body,
        mesh=mesh,
        in_specs=placed,
        out_specs=(
            P(("dp", "expert"), "context", None),
            P(("dp", "expert"), "context", None),
            P("context"),
            P("context", None),
            P("context", None),
            P("context"),
            P("expert", "context", None),
            P("expert", "context", None),
        ),
        check_vma=False,
    )
```

profile of v0, /device:TPU:0, one launch (start us, length us, event | category | flops | bytes accessed | tf_op | source)
XLA Modules:
  0.0 1118.1 jit_solution(16908174951950881660)
XLA Ops:
  8.6 4.9 fusion.92
  18.6 18.0 %all_gather.8 = bf16[1024,2,128]{0,2,1:T(8,128)(2,1)} all-gather(bf16[256,2,128]{0,2,1:T(8,128)(2,1)S(1)} %pad_maximum_fusion.6), channel_id=1, replica_groups=mesh['dp'=2,'context'=4,'expert'=4] {'context'}, dimensions={0}, use_global_device_ids=true | all-gather | bytes 655360 | tf_op jit(solution)/shard_map/all_gather | solution.py:187
  36.6 17.2 %all_gather.9 = bf16[1024,2,128]{2,0,1:T(8,128)(2,1)} all-gather(bf16[256,2,128]{2,0,1:T(8,128)(2,1)S(1)} %copy-done.20), channel_id=1, replica_groups=mesh['dp'=2,'context'=4,'expert'=4] {'context'}, dimensions={0}, use_global_device_ids=true | all-gather | bytes 655360 | tf_op jit(solution)/shard_map/all_gather | solution.py:188
  54.4 14.9 %conditional.2 = (f32[2,6,256]{2,1,0:T(8,128)S(1)}, f32[2,6,256,128]{3,2,1,0:T(8,128)S(1)}, f32[2,6,256]{2,1,0:T(8,128)S(1)}) conditional(s32[]{:T(128)} %convert_element_type.184, (f32[2,6,256]{2,1,0:T(8,128)S(1)}, f32[2,6,256]{2,1,0:T(8,128)S(1)}, f32[2,6,256,128]{3,2,1,0:T(8,128)S(1)}) %tuple.53, (s32[256]{0:T(256)S(1)}, ...), branch_computations={%region_2.3_spmd.clone, %region_3.6_spmd.clone} | conditional | flops 1646797824 | bytes 94296120 | solution.py:205
  62.5 6.8 multiply_add_fusion
  73.6 4.1 multiply_reduce_fusion.4
  80.4 5.9 reshape.291
  89.4 9.3 scatter_custom_fusion
  98.7 5.5 all-to-all-start
  104.4 3.7 mul.448
  108.1 7.7 mul.449
  116.1 9.9 scatter_custom_fusion.1
  126.0 32.0 %all-to-all-done = bf16[4,2,192,1536]{3,2,1,0:T(8,128)(2,1)} async-done(((bf16[4,2,192,1536]{3,2,1,0:T(8,128)(2,1)}), bf16[4,2,192,1536]{3,2,1,0:T(8,128)(2,1)}, u32[]{:S(2)}, u32[]{:S(2)}) %all-to-all-start) | async-done | bytes 4718624 | tf_op jit(solution)/shard_map/all_to_all | solution.py:229
  158.0 5.1 all-to-all-start.2
  163.1 14.2 %fusion.46 = f32[4,2,192,1536]{3,2,0,1:T(8,128)} fusion(bf16[2,1536,1536]{2,1,0:T(8,128)(2,1)} %param.25, bf16[4,2,192,1536]{3,2,1,0:T(8,128)(2,1)} %all-to-all-done), kind=kOutput, calls=%fused_computation.70 | convolution fusion | flops 7247757312 | bytes 23592960 | tf_op jit(solution)/shard_map/sjcd,jdf->sjcf/dot_general | solution.py:230
  177.3 39.6 %all-to-all-done.2 = bf16[4,2,192,1536]{3,2,1,0:T(8,128)(2,1)} async-done(((bf16[4,2,192,1536]{3,2,1,0:T(8,128)(2,1)}), bf16[4,2,192,1536]{3,2,1,0:T(8,128)(2,1)}, u32[]{:S(2)}, u32[]{:S(2)}) %all-to-all-start.2) | async-done | bytes 4718624 | tf_op jit(solution)/shard_map/all_to_all | solution.py:254
  217.0 12.8 %fusion.55 = (bf16[4,2,192,768]{3,2,0,1:T(8,128)(2,1)}, bf16[4,2,192,768]{3,2,0,1:T(8,128)(2,1)}, bf16[4,2,192,768]{3,2,0,1:T(8,128)(2,1)S(1)}) fusion(f32[4,2,192,1536]{3,2,0,1:T(8,128)} %fusion.46, bf16[2,768,1536]{2,1,0:T(8,128)(2,1)} %param.26, bf16[4,2,192,1536]{3,2,1,0:T(8,128)(2,1)} %all-to-all-done.2), kind=kOutput, calls=%fused_computation.77 | convolution fusion | flops 3654549504 | bytes 25952256 | tf_op jit(solution)/shard_map/sjcd,jfd->sjcf/dot_general | solution.py:259
  229.8 7.2 convert_bitcast_fusion.1
  239.5 4.9 all-to-all-start.1
  244.4 11.5 %convert_bitcast_fusion = bf16[4,2,192,1536]{3,2,0,1:T(8,128)(2,1)S(1)} fusion(bf16[2,1536,1536]{2,1,0:T(8,128)(2,1)} %param.25, bf16[4,2,192,768]{3,2,0,1:T(8,128)(2,1)} %get-tuple-element.575, bf16[4,2,192,768]{3,2,0,1:T(8,128)(2,1)} %get-tuple-element.574), kind=kOutput, calls=%fused_computation.88 | convolution fusion | flops 7259553792 | bytes 18874368 | tf_op jit(solution)/shard_map/sjcf,jdf->sjcd/dot_general | solution.py:270
  258.4 39.8 %all-to-all-done.1 = bf16[4,2,192,1536]{3,2,1,0:T(8,128)(2,1)} async-done(((bf16[4,2,192,1536]{3,2,1,0:T(8,128)(2,1)}), bf16[4,2,192,1536]{3,2,1,0:T(8,128)(2,1)}, u32[]{:S(2)}, u32[]{:S(2)}) %all-to-all-start.1) | async-done | bytes 4718624 | tf_op jit(solution)/shard_map/all_to_all | solution.py:235
  298.3 5.0 all-to-all-start.3
  305.5 23.2 %gather_fusion = bf16[1024,1536]{1,0:T(8,128)(2,1)} fusion(bf16[8,192,1536]{2,1,0:T(8,128)(2,1)} %bitcast.30, s32[1024]{0:T(1024)S(1)} %bitcast.194), kind=kCustom, calls=%fused_computation | custom fusion | bytes 6299648 | tf_op jit(solution)/shard_map/gather | solution.py:239
  328.7 6.7 reshape.274
  335.4 21.7 %all-to-all-done.3 = bf16[4,2,192,1536]{3,2,1,0:T(8,128)(2,1)} async-done(((bf16[4,2,192,1536]{3,2,1,0:T(8,128)(2,1)}), bf16[4,2,192,1536]{3,2,1,0:T(8,128)(2,1)}, u32[]{:S(2)}, u32[]{:S(2)}) %all-to-all-start.3) | async-done | bytes 4718624 | tf_op jit(solution)/shard_map/all_to_all | solution.py:273
  357.1 23.2 %gather_fusion.1 = bf16[1024,1536]{1,0:T(8,128)(2,1)} fusion(bf16[8,192,1536]{2,1,0:T(8,128)(2,1)} %bitcast.40, s32[1024]{0:T(1024)S(1)} %bitcast.195), kind=kCustom, calls=%fused_computation.1 | custom fusion | bytes 6299648 | tf_op jit(solution)/shard_map/gather | solution.py:276
  380.3 7.1 reshape.276
  387.5 7.7 reduce_sum.106
  397.0 7.5 multiply_reduce_fusion
  407.2 4.8 convolution_convert_fusion.2
  416.5 16.6 %while.5 = (s32[]{:T(128)}, bf16[1024,2,128]{0,2,1:T(8,128)(2,1)}, bf16[1024,2,128]{0,2,1:T(8,128)(2,1)}, f32[2,6,256,128]{3,2,1,0:T(8,128)}, s32[]{:T(128)}, /*...) while((s32[]{:T(128)}, bf16[1024,2,128]{0,2,1:T(8,128)(2,1)}, ...), condition=%wide.region_19.20_spmd.clone, body=%wide.region_16.19_spmd.clone.sunk | while | flops 2030830336 | bytes 44744052 | solution.py:337
  416.6 9.7 conditional.5
  433.9 5.2 convolution_convert_fusion.1
  441.4 22.6 %reduce-scatter.7.cloned.1.call-done = bf16[256,2,128]{0,2,1:T(8,128)(2,1)} async-done(((bf16[1024,2,128]{0,2,1:T(8,128)(2,1)}), bf16[256,2,128]{0,2,1:T(8,128)(2,1)}) %reduce-scatter.7.cloned.1.call-update) | async-done | bytes 131088 | tf_op jit(solution)/shard_map/reduce_scatter | solution.py:339
  465.0 21.0 %reduce-scatter.9.cloned.1.call-done = bf16[256,2,128]{0,2,1:T(8,128)(2,1)} async-done(((bf16[1024,2,128]{0,2,1:T(8,128)(2,1)}), bf16[256,2,128]{0,2,1:T(8,128)(2,1)}) %reduce-scatter.9.cloned.1.call-update) | async-done | bytes 131088 | tf_op jit(solution)/shard_map/reduce_scatter | solution.py:342
  486.0 5.5 convolution_convert_fusion
  491.8 10.0 bitcast_convert_fusion.1
  501.9 13.2 %bitcast_convert_fusion = bf16[2,1536,1536]{2,1,0:T(8,128)(2,1)} fusion(bf16[4,2,192,1536]{3,2,1,0:T(8,128)(2,1)} %all-to-all-done, bf16[4,2,192,768]{3,2,0,1:T(8,128)(2,1)} %get-tuple-element.575, bf16[4,2,192,768]{3,2,0,1:T(8,128)(2,1)} %get-tuple-element.574), kind=kOutput, calls=%fused_computation.58 | convolution fusion | flops 7261913088 | bytes 18874368 | tf_op jit(solution)/shard_map/sjcd,sjcf->jdf/dot_general | solution.py:267
  515.2 57.3 %reduce-scatter.13.cloned.1.call-done = bf16[384,1536]{1,0:T(8,128)(2,1)} async-done(((bf16[1536,1536]{1,0:T(8,128)(2,1)}), bf16[384,1536]{1,0:T(8,128)(2,1)}) %reduce-scatter.13.cloned.1.call-update) | async-done | bytes 1179664 | tf_op jit(solution)/shard_map/reduce_scatter | solution.py:377
  572.4 113.5 %reduce-scatter.11.cloned.1.call-done = bf16[384,2048]{1,0:T(8,128)(2,1)} async-done(((bf16[1536,2048]{1,0:T(8,128)(2,1)}), bf16[384,2048]{1,0:T(8,128)(2,1)}) %reduce-scatter.11.cloned.1.call-update) | async-done | bytes 1572880 | tf_op jit(solution)/shard_map/reduce_scatter | solution.py:374
  686.0 87.9 %reduce-scatter.17.cloned.1.call-done = bf16[2,192,1536]{2,1,0:T(8,128)(2,1)} async-done(((bf16[2,768,1536]{2,1,0:T(8,128)(2,1)}), bf16[2,192,1536]{2,1,0:T(8,128)(2,1)}) %reduce-scatter.17.cloned.1.call-update) | async-done | bytes 1179664 | tf_op jit(solution)/shard_map/reduce_scatter | solution.py:386
  773.8 164.1 %reduce-scatter.15.cloned.1.call-done = bf16[2,384,1536]{2,1,0:T(8,128)(2,1)} async-done(((bf16[2,1536,1536]{2,1,0:T(8,128)(2,1)}), bf16[2,384,1536]{2,1,0:T(8,128)(2,1)}) %reduce-scatter.15.cloned.1.call-update) | async-done | bytes 2359312 | tf_op jit(solution)/shard_map/reduce_scatter | solution.py:383
  939.2 6.1 fusion.85
  945.3 11.4 %all-reduce.4 = (bf16[1536]{0:T(1024)(128)(2,1)S(1)}, bf16[1536]{0:T(1024)(128)(2,1)S(1)}) all-reduce(bf16[1536]{0:T(1024)(128)(2,1)S(1)} %get-tuple-element.531, bf16[1536]{0:T(1024)(128)(2,1)S(1)} %get-tuple-element.529), channel_id=4, replica_groups=mesh['dp'=2,'context'=4,'expert'=4] {'context'}, use_global_device_ids=true, to_apply=%region_24.25.clone | all-reduce | flops 3072 | bytes 12288
  956.8 11.9 %all-reduce.2 = (bf16[384]{0:T(512)(128)(2,1)S(1)}, bf16[384]{0:T(512)(128)(2,1)S(1)}) all-reduce(bf16[384]{0:T(512)(128)(2,1)S(1)} %dynamic-slice.1, bf16[384]{0:T(512)(128)(2,1)S(1)} %dynamic-slice.3), channel_id=1, replica_groups=mesh['dp'=2,'context'=4,'expert'=4] {'dp','expert'}, use_global_device_ids=true, to_apply=%region_25.26 | all-reduce | flops 768 | bytes 3072 | tf_op jit(solution)/shard_map/psum | solution.py:396
  972.9 35.1 %all-reduce.9.cloned.1.call-done = (bf16[384,2048]{1,0:T(8,128)(2,1)}, bf16[384,1536]{1,0:T(8,128)(2,1)}) async-done(((bf16[384,2048]{1,0:T(8,128)(2,1)}, bf16[384,1536]{1,0:T(8,128)(2,1)}), (bf16[384,2048]{1,0:T(8,128)(2,1)}, bf16[384,1536]{1,0:T(8,128)(2,1)})) %all-reduce.9.cloned.1.call-update) | async-done | bytes 2752528 | tf_op jit(solution)/shard_map/psum | solution.py:397
  1013.3 91.4 %all-reduce.11.cloned.1.call-done = (bf16[2,384,1536]{2,1,0:T(8,128)(2,1)}, bf16[2,192,1536]{2,1,0:T(8,128)(2,1)}) async-done(((bf16[2,384,1536]{2,1,0:T(8,128)(2,1)}, bf16[2,192,1536]{2,1,0:T(8,128)(2,1)}), (bf16[2,384,1536]{2,1,0:T(8,128)(2,1)}, bf16[2,192,1536]{2,1,0:T(8,128)(2,1)})) %all-reduce.11.cloned.1.call-update) | async-done | bytes 3538960 | tf_op jit(solution)/shard_map/psum | solution.py:392
  1104.7 4.6 convert_element_type.222
  (186 shorter events, 74.3 us)
Async XLA Ops:
  8.6 4.9 copy-start.24
  13.5 1.3 copy-start.12
  13.5 2.0 copy-start.29
  13.5 2.5 copy-start.30
  16.0 0.6 copy-start.27
  17.1 1.4 slice-start
  17.4 19.2 %copy-start.13 = (f32[256,64]{0,1:T(8,128)}, f32[256,64]{0,1:T(8,128)S(1)}, u32[]{:S(2)}) copy-start(f32[256,64]{0,1:T(8,128)S(1)} %get-tuple-element.590) | copy-start | bytes 196612
  17.4 19.2 %copy-start.15 = (f32[256,64]{0,1:T(8,128)}, f32[256,64]{0,1:T(8,128)S(1)}, u32[]{:S(2)}) copy-start(f32[256,64]{0,1:T(8,128)S(1)} %get-tuple-element.591) | copy-start | bytes 196612
  17.6 19.0 %copy-start.20 = (bf16[256,2,128]{2,0,1:T(8,128)(2,1)S(1)}, bf16[256,2,128]{2,0,1:T(8,128)(2,1)}, u32[]{:S(2)}) copy-start(bf16[256,2,128]{2,0,1:T(8,128)(2,1)} %copy_bitcast_fusion) | copy-start | bytes 393220
  18.6 35.9 %copy-start.28 = (s32[256]{0:T(256)S(1)}, s32[256]{0:T(256)}, u32[]{:S(2)}) copy-start(s32[256]{0:T(256)} %copy-done.27) | copy-start | bytes 3076
  57.9 4.5 copy-start.1
  69.3 1.1 copy-start.10
  70.5 3.1 copy-start.3
  72.4 1.2 copy-start.5
  73.6 4.1 copy-start.2
  73.6 4.1 copy-start.22
  80.4 8.8 copy-start.32
  80.4 8.9 copy-start.31
  98.7 5.5 copy-start.11
  98.7 59.3 %all-to-all-start = ((bf16[4,2,192,1536]{3,2,1,0:T(8,128)(2,1)}), bf16[4,2,192,1536]{3,2,1,0:T(8,128)(2,1)}, u32[]{:S(2)}, u32[]{:S(2)}) async-start(bf16[4,2,192,1536]{3,2,1,0:T(8,128)(2,1)} %bitcast.197), calls=%async_computation | async-start | bytes 9437184 | tf_op jit(solution)/shard_map/all_to_all | solution.py:229
  108.1 7.7 copy-start.26
  158.0 59.0 %all-to-all-start.2 = ((bf16[4,2,192,1536]{3,2,1,0:T(8,128)(2,1)}), bf16[4,2,192,1536]{3,2,1,0:T(8,128)(2,1)}, u32[]{:S(2)}, u32[]{:S(2)}) async-start(bf16[4,2,192,1536]{3,2,1,0:T(8,128)(2,1)} %bitcast.198), calls=%async_computation.2 | async-start | bytes 9437184 | tf_op jit(solution)/shard_map/all_to_all | solution.py:254
  229.8 7.2 copy-start.34
  239.5 58.8 %all-to-all-start.1 = ((bf16[4,2,192,1536]{3,2,1,0:T(8,128)(2,1)}), bf16[4,2,192,1536]{3,2,1,0:T(8,128)(2,1)}, u32[]{:S(2)}, u32[]{:S(2)}) async-start(bf16[4,2,192,1536]{3,2,1,0:T(8,128)(2,1)} %copy.97), calls=%async_computation.1 | async-start | bytes 9437184 | tf_op jit(solution)/shard_map/all_to_all | solution.py:235
  298.3 58.8 %all-to-all-start.3 = ((bf16[4,2,192,1536]{3,2,1,0:T(8,128)(2,1)}), bf16[4,2,192,1536]{3,2,1,0:T(8,128)(2,1)}, u32[]{:S(2)}, u32[]{:S(2)}) async-start(bf16[4,2,192,1536]{3,2,1,0:T(8,128)(2,1)} %copy.100), calls=%async_computation.3 | async-start | bytes 9437184 | tf_op jit(solution)/shard_map/all_to_all | solution.py:273
  303.3 160.7 %reduce-scatter.7.cloned.1.call-start = ((), (), s32[]{:S(2)}) async-start(), calls=%async_computation.10 | async-start | bytes 655360 | tf_op jit(solution)/shard_map/reduce_scatter | solution.py:339
  397.0 7.5 copy-start.9
  406.1 1.1 copy-start.7
  407.2 6.2 copy-start.6
  416.7 2.2 copy-start.19
  433.1 52.9 %reduce-scatter.9.cloned.1.call-start = ((), (), s32[]{:S(2)}) async-start(), calls=%async_computation.11 | async-start | bytes 655360 | tf_op jit(solution)/shard_map/reduce_scatter | solution.py:342
  433.9 138.5 %reduce-scatter.13.cloned.1.call-start = ((), (), s32[]{:S(2)}) async-start(), calls=%async_computation.13 | async-start | bytes 5898240 | tf_op jit(solution)/shard_map/reduce_scatter | solution.py:377
  439.1 1.4 copy-start
  439.1 1.9 copy-start.14
  439.2 1.9 copy-start.16
  439.2 246.7 %reduce-scatter.11.cloned.1.call-start = ((), (), s32[]{:S(2)}) async-start(), calls=%async_computation.12 | async-start | bytes 7864320 | tf_op jit(solution)/shard_map/reduce_scatter | solution.py:374
  441.0 45.0 %copy-start.4 = (bf16[1,256,1536]{2,1,0:T(8,128)(2,1)S(1)}, bf16[1,256,1536]{2,1,0:T(8,128)(2,1)}, u32[]{:S(2)}) copy-start(bf16[1,256,1536]{2,1,0:T(8,128)(2,1)} %param.17) | copy-start | bytes 2359300
  441.0 45.0 %copy-start.23 = (f32[1536]{0:T(1024)S(1)}, f32[1536]{0:T(1024)}, u32[]{:S(2)}) copy-start(f32[1536]{0:T(1024)} %param.21) | copy-start | bytes 18436
  441.1 45.0 %copy-start.25 = (f32[256]{0:T(256)S(1)}, f32[256]{0:T(256)}, u32[]{:S(2)}) copy-start(f32[256]{0:T(256)} %copy-done.24) | copy-start | bytes 3076
  491.6 282.3 %reduce-scatter.17.cloned.1.call-start = ((), (), s32[]{:S(2)}) async-start(), calls=%async_computation.15 | async-start | bytes 5898240 | tf_op jit(solution)/shard_map/reduce_scatter | solution.py:386
  501.9 436.0 %reduce-scatter.15.cloned.1.call-start = ((), (), s32[]{:S(2)}) async-start(), calls=%async_computation.14 | async-start | bytes 11796480 | tf_op jit(solution)/shard_map/reduce_scatter | solution.py:383
  515.1 492.9 %all-reduce.9.cloned.1.call-start = ((), (), s32[]{:S(2)}) async-start(), calls=%async_computation.16 | async-start | bytes 5505024 | tf_op jit(solution)/shard_map/psum | solution.py:397
  685.9 252.1 %copy-start.33 = (u32[32]{0:T(128)S(1)}, u32[32]{0:T(128)}, u32[]{:S(2)}) copy-start(u32[32]{0:T(128)} %constant.175) | copy-start | bytes 388
  685.9 253.3 %copy-start.21 = (bf16[256,2,128]{0,2,1:T(8,128)(2,1)S(1)}, bf16[256,2,128]{0,2,1:T(8,128)(2,1)}, u32[]{:S(2)}) copy-start(bf16[256,2,128]{0,2,1:T(8,128)(2,1)} %reduce-scatter.9.cloned.1.call-done) | copy-start | bytes 393220
  685.9 418.8 %all-reduce.11.cloned.1.call-start = ((), (), s32[]{:S(2)}) async-start(), calls=%async_computation.17 | async-start | bytes 7077888 | tf_op jit(solution)/shard_map/psum | solution.py:392
  939.2 30.7 %copy-start.8 = (f32[256,1536]{1,0:T(8,128)S(1)}, f32[256,1536]{1,0:T(8,128)}, u32[]{:S(2)}) copy-start(f32[256,1536]{1,0:T(8,128)} %copy-done.7) | copy-start | bytes 4718596
  1008.0 3.5 copy-start.17
  1104.7 4.6 copy-start.18
Sparse Core Ops, SparseCore 0:
  433.2 30.7 reduce-scatter.6
  466.3 19.7 reduce-scatter.8
  488.9 83.4 reduce-scatter.12
  574.6 111.2 reduce-scatter.10
  688.0 85.7 reduce-scatter.16
  776.0 161.8 reduce-scatter.14
  941.2 66.7 all-reduce.8
  1010.3 94.3 all-reduce.10
where the time goes:
time: 1130 us; the launch traced here: 1120 us
  waiting for transfers between devices  727 us (64%)
  matrix products  119 us (11%)
  local copies, waits for them, and re-layouts  118 us (10%)
  other arithmetic  58.6 us (5%)
  blocking collectives  58.4 us (5%)
  starting transfers between devices  21.1 us (2%)
  between operations  15.7 us (1%)
    reduce_scatter x1, waiting for transfers between devices, body(): lax.psum_scatter(gate_up_grad.astype(jnp.bfloat16), 'context', scatter_di...  164 us
    reduce_scatter x1, waiting for transfers between devices, body(): lax.psum_scatter(qkv_grad.astype(jnp.bfloat16), 'context', scatter_dimens...  113 us
    psum x1, waiting for transfers between devices, body(): lax.psum(summed[4].astype(jnp.bfloat16), 'dp').astype(jnp.float32)  91.4 us
    reduce_scatter x1, waiting for transfers between devices, body(): lax.psum_scatter(down_grad.astype(jnp.bfloat16), 'context', scatter_dimen...  87.9 us
    reduce_scatter x1, waiting for transfers between devices, body(): lax.psum_scatter(out_proj_grad.astype(jnp.bfloat16), 'context', scatter_d...  57.3 us
    all_to_all x1, waiting for transfers between devices, body(): lax.all_to_all(produced.astype(jnp.bfloat16), 'expert', split_axis=0, con...  39.8 us
    all_to_all x1, waiting for transfers between devices, body(): lax.all_to_all(grad_send, 'expert', split_axis=0, concat_axis=0, tiled=True)  39.6 us
    psum x1, waiting for transfers between devices, body(): lax.psum(dense_rows[1].astype(jnp.bfloat16), ('dp', 'expert'))  35.1 us
  transfers between devices with their start and end apart: 12, of which 12 were waited for; matrix products, arithmetic and copies ran while one was open for 12% of the time, Pallas kernels for 0%

commit v1 on v0

--- a/solution.py
+++ b/solution.py
@@ -1,6 +1,8 @@
 import jax
 import jax.numpy as jnp
 from jax import lax
+from jax.experimental import pallas as pl
+from jax.experimental.pallas import tpu as pltpu
 from jax.sharding import PartitionSpec as P
 
 D = 1536
@@ -410,7 +412,658 @@
     )
 
 
+MESH = pl.DeviceIdType.MESH
+BF = jnp.bfloat16
+F32 = jnp.float32
+NN = (((1,), (0,)), ((), ()))
+NT = (((1,), (1,)), ((), ()))
+TN = (((0,), (0,)), ((), ()))
+
+
+def matmul(left, right, dims=NN):
+    return lax.dot_general(left, right, dims, preferred_element_type=F32)
+
+
+def flip(axis, bit):
+    index = lax.axis_index(axis)
+    return {axis: index + bit - 2 * bit * ((index // bit) % 2)}
+
+
+def greet(peers):
+    barrier = pltpu.get_barrier_semaphore()
+    for peer in peers:
+        pl.semaphore_signal(barrier, inc=1, device_id=peer, device_id_type=MESH)
+    pl.semaphore_wait(barrier, len(peers))
+
+
+def remote(src, dst, send_sem, recv_sem, peer):
+    return pltpu.make_async_remote_copy(
+        src_ref=src,
+        dst_ref=dst,
+        send_sem=send_sem,
+        recv_sem=recv_sem,
+        device_id=peer,
+        device_id_type=MESH,
+    )
+
+
+def other(axis, distance):
+    size = lax.axis_size(axis)
+    return {axis: lax.rem(lax.axis_index(axis) + distance, size)}
+
+
+def mate(code):
+    expert = lax.axis_index("expert")
+    for bit in (1, 2):
+        if code & bit:
+            expert = expert + bit - 2 * bit * ((expert // bit) % 2)
+    return {**flip("dp", 1), "expert": expert} if code & 4 else {"expert": expert}
+
+
+class GroupGather:
+    def __init__(self, own, held, sems, rows):
+        half = rows // 2
+        self.x, self.y, self.core = flip("dp", 1), flip("expert", 2), flip("expert", 1)
+
+        def part(which, index, amount=1):
+            return held.at[pl.ds(which * 2 * rows + index * half, amount * half)]
+
+        def link(number, src, dst, peer):
+            return remote(src, dst, sems.at[0, number], sems.at[1, number], peer)
+
+        first, second = own.at[pl.ds(0, half)], own.at[pl.ds(half, half)]
+        self.links = [
+            link(0, first, part(1, 0), self.x),
+            link(1, second, part(1, 1), self.y),
+            link(2, first, part(2, 0), self.y),
+            link(3, second, part(2, 1), self.x),
+            link(4, part(1, 0), part(3, 0), self.y),
+            link(5, part(1, 1), part(3, 1), self.x),
+        ]
+        self.cores = [link(6, own, part(0, 2, 2), self.core)]
+        for which in range(1, 4):
+            self.cores.append(
+                link(6 + which, part(which, 0, 2), part(which, 2, 2), self.core)
+            )
+
+    def start(self):
+        self.cores[0].start()
+        for link in self.links[:4]:
+            link.start()
+
+    def forward(self, which):
+        for link in self.links[2 * which - 2 : 2 * which]:
+            link.wait_recv()
+        if which == 1:
+            for link in self.links[4:]:
+                link.start()
+        self.cores[which].start()
+
+    def arrived(self, which):
+        self.cores[which].wait_recv()
+
+    def finish(self):
+        for link in self.links + self.cores:
+            link.wait_send()
+
+
+GATHER_SEMS = pltpu.SemaphoreType.DMA((2, 10))
+
+
+def rotate(values, cosine, sine):
+    return values * cosine + pltpu.roll(values, values.shape[1] // 2, 1) * sine
+
+
+def attention_kernel(
+    x_ref,
+    share_ref,
+    begin_ref,
+    cos_ref,
+    sin_ref,
+    attn_gain_ref,
+    ffn_gain_ref,
+    c_ref,
+    w_qkv_ref,
+    w_out_ref,
+    h1_ref,
+    q_ref,
+    att_ref,
+    logsum_ref,
+    merged_ref,
+    residual_ref,
+    h2_ref,
+    kv_ref,
+    c_all_ref,
+    share_all_ref,
+    w_qkv,
+    w_out,
+    kv,
+    accumulated,
+    top,
+    total,
+    bias,
+    load_sems,
+    kv_sems,
+    share_sems,
+    gather_sems,
+):
+    contexts = lax.axis_size("context")
+    me = lax.axis_index("context")
+    rows = x_ref.shape[0]
+    query_width = QUERY_HEADS * HEAD_SIZE
+    heads = QUERY_HEADS // KEY_VALUE_HEADS
+    scaling = HEAD_SIZE ** (-0.5)
+
+    loads = [
+        pltpu.make_async_copy(
+            w_qkv_ref.at[:, query_width:], w_qkv.at[:, query_width:], load_sems.at[0]
+        ),
+        pltpu.make_async_copy(
+            w_qkv_ref.at[:, :query_width], w_qkv.at[:, :query_width], load_sems.at[1]
+        ),
+        pltpu.make_async_copy(w_out_ref, w_out, load_sems.at[2]),
+        pltpu.make_async_copy(c_ref, c_all_ref.at[pl.ds(0, rows)], load_sems.at[3]),
+        pltpu.make_async_copy(share_ref, share_all_ref.at[0], load_sems.at[4]),
+    ]
+    for load in loads:
+        load.start()
+
+    mates = [mate(code) for code in range(1, 8)]
+    greet([other("context", step) for step in range(1, contexts)] + mates)
+
+    gather = GroupGather(c_ref, c_all_ref, gather_sems, rows)
+    gather.start()
+    shares = [
+        remote(
+            share_ref,
+            share_all_ref.at[1 + index],
+            share_sems.at[0, index],
+            share_sems.at[1, index],
+            mate,
+        )
+        for index, mate in enumerate(mates)
+    ]
+    for share in shares:
+        share.start()
+
+    x = x_ref[...].astype(F32)
+    inverse = lax.rsqrt(jnp.mean(x * x, axis=-1, keepdims=True) + epsilon)
+    h1_ref[...] = (x * inverse * attn_gain_ref[...]).astype(BF)
+
+    loads[0].wait()
+    projected = matmul(h1_ref[...], w_qkv[:, query_width:])
+    for head in range(KEY_VALUE_HEADS):
+        lanes = slice(head * HEAD_SIZE, (head + 1) * HEAD_SIZE)
+        kv[me, :, lanes] = rotate(projected[:, lanes], cos_ref[...], sin_ref[...]).astype(BF)
+    kv[me, :, KEY_VALUE_HEADS * HEAD_SIZE :] = projected[:, KEY_VALUE_HEADS * HEAD_SIZE :].astype(
+        BF
+    )
+
+    def kv_copy(step):
+        return remote(
+            kv.at[me],
+            kv.at[me],
+            kv_sems.at[0, step],
+            kv_sems.at[1, step],
+            {"context": lax.rem(me + step, contexts)},
+        )
+
+    for step in range(1, contexts):
+
+        @pl.when(me + step < contexts)
+        def _():
+            kv_copy(step).start()
+
+    loads[1].wait()
+    chunk = 4 * HEAD_SIZE
+    for offset in range(0, query_width, chunk):
+        projected = matmul(h1_ref[...], w_qkv[:, offset : offset + chunk])
+        for head in range(chunk // HEAD_SIZE):
+            lanes = slice(head * HEAD_SIZE, (head + 1) * HEAD_SIZE)
+            q_ref[offset // HEAD_SIZE + head] = rotate(
+                projected[:, lanes], cos_ref[...], sin_ref[...]
+            ).astype(BF)
+
+    top[...] = jnp.full_like(top, negative_huge)
+    total[...] = jnp.zeros_like(total)
+    accumulated[...] = jnp.zeros_like(accumulated)
+    query_pos = me * rows + lax.broadcasted_iota(jnp.int32, (rows, rows), 1)
+    begin_row = begin_ref[...]
+
+    def fold(block):
+        key_pos = block * rows + lax.broadcasted_iota(jnp.int32, (rows, rows), 0)
+        allowed = (key_pos <= query_pos) & (key_pos >= begin_row)
+        bias[...] = jnp.where(allowed, 0.0, negative_huge)
+        for head in range(QUERY_HEADS):
+            group = head // heads
+            keys = kv[block, :, group * HEAD_SIZE : (group + 1) * HEAD_SIZE]
+            values = kv[
+                block,
+                :,
+                (KEY_VALUE_HEADS + group) * HEAD_SIZE : (KEY_VALUE_HEADS + group + 1) * HEAD_SIZE,
+            ]
+            scores = matmul(keys, q_ref[head], NT) * scaling + bias[...]
+            old = top[head : head + 1]
+            new = jnp.maximum(old, jnp.max(scores, axis=0, keepdims=True))
+            weights = jnp.exp(scores - new)
+            shrink = jnp.exp(old - new)
+            top[head : head + 1] = new
+            total[head : head + 1] = total[head : head + 1] * shrink + jnp.sum(
+                weights, axis=0, keepdims=True
+            )
+            accumulated[head] = accumulated[head] * shrink + matmul(
+                values, weights.astype(BF), TN
+            )
+
+    fold(me)
+
+    def earlier(step, carry):
+        kv_arrival(step).wait_recv()
+        fold(me - step)
+        return carry
+
+    def kv_arrival(step):
+        return remote(
+            kv.at[me],
+            kv.at[lax.rem(me - step + contexts, contexts)],
+            kv_sems.at[0, step],
+            kv_sems.at[1, step],
+            {"context": lax.rem(me + step, contexts)},
+        )
+
+    gather.forward(1)
+    lax.fori_loop(1, me + 1, earlier, 0)
+    gather.forward(2)
+
+    loads[2].wait()
+    for head in range(QUERY_HEADS):
+        attended = accumulated[head] / total[head : head + 1]
+        att_ref[head] = attended
+        merged_ref[:, head * HEAD_SIZE : (head + 1) * HEAD_SIZE] = attended.T.astype(BF)
+    logsum_ref[...] = jnp.where(total[...] > 0, top[...] + jnp.log(total[...]), 0.0)
+    residual = x_ref[...].astype(F32) + matmul(merged_ref[...], w_out[...])
+    residual_ref[...] = residual
+    inverse = lax.rsqrt(jnp.mean(residual * residual, axis=-1, keepdims=True) + epsilon)
+    h2_ref[...] = (residual * inverse * ffn_gain_ref[...]).astype(BF)
+
+    def keep(block, carry):
+        copy = pltpu.make_async_copy(kv.at[block], kv_ref.at[block], load_sems.at[5])
+        copy.start()
+        copy.wait()
+        return carry
+
+    lax.fori_loop(0, me + 1, keep, 0)
+    gather.forward(3)
+    for which in range(4):
+        gather.arrived(which)
+    gather.finish()
+    for share in shares:
+        share.wait()
+    loads[3].wait()
+    loads[4].wait()
+    for step in range(1, contexts):
+
+        @pl.when(me + step < contexts)
+        def _():
+            kv_copy(step).wait_send()
+
+
+VM = pl.BlockSpec(memory_space=pltpu.VMEM)
+ANY = pl.BlockSpec(memory_space=pl.ANY)
+
+
+def attention_forward(
+    x, share, begins, cosine, sine, attn_gain, ffn_gain, cotangent, w_qkv, w_out
+):
+    rows = x.shape[0]
+    contexts = lax.axis_size("context")
+    group = lax.axis_size("dp") * lax.axis_size("expert")
+    kv_width = 2 * KEY_VALUE_HEADS * HEAD_SIZE
+    padded = -(-QUERY_HEADS // 8) * 8
+    shape = jax.ShapeDtypeStruct
+    return pl.pallas_call(
+        attention_kernel,
+        out_shape=[
+            shape((rows, D), BF),
+            shape((QUERY_HEADS, rows, HEAD_SIZE), BF),
+            shape((QUERY_HEADS, HEAD_SIZE, rows), F32),
+            shape((padded, rows), F32),
+            shape((rows, D), BF),
+            shape((rows, D), F32),
+            shape((rows, D), BF),
+            shape((contexts, rows, kv_width), BF),
+            shape((group * rows, D), BF),
+            shape((group,) + share.shape, F32),
+        ],
+        in_specs=[VM] * 7 + [ANY] * 3,
+        out_specs=[VM] * 7 + [ANY] * 3,
+        scratch_shapes=[
+            pltpu.VMEM(w_qkv.shape, BF),
+            pltpu.VMEM(w_out.shape, BF),
+            pltpu.VMEM((contexts, rows, kv_width), BF),
+            pltpu.VMEM((QUERY_HEADS, HEAD_SIZE, rows), F32),
+            pltpu.VMEM((padded, rows), F32),
+            pltpu.VMEM((padded, rows), F32),
+            pltpu.VMEM((rows, rows), F32),
+            pltpu.SemaphoreType.DMA((6,)),
+            pltpu.SemaphoreType.DMA((2, contexts)),
+            pltpu.SemaphoreType.DMA((2, group - 1)),
+            GATHER_SEMS,
+        ],
+        compiler_params=pltpu.CompilerParams(
+            collective_id=0, has_side_effects=True, vmem_limit_bytes=56 << 20
+        ),
+        cost_estimate=pl.CostEstimate(
+            flops=2 * rows * D * 4096, bytes_accessed=30 << 20, transcendentals=rows * rows * 12
+        ),
+    )(x, share, begins, cosine, sine, attn_gain, ffn_gain, cotangent, w_qkv, w_out)
+
+
+def prepare(routes, gates, doc_starts, rows, expert_total):
+    positions = lax.axis_index("context") * rows + jnp.arange(rows, dtype=jnp.int32)
+    begins = doc_begins(positions, doc_starts[0])
+    cosine, sine = rope_tables(positions - begins, HEAD_SIZE // 2)
+    cosine = jnp.concatenate([cosine, cosine], axis=1)
+    sine = jnp.concatenate([-sine, sine], axis=1)
+    named = routes[0][None] == jnp.arange(expert_total, dtype=jnp.int32)[:, None, None]
+    share = jnp.sum(jnp.where(named, gates[0][None], 0.0), axis=2)
+    return begins[None, :], cosine, sine, share
+
+
+SLOT_CODES = ((0, 0, 1, 1), (4, 2, 5, 3), (2, 4, 3, 5), (6, 6, 7, 7))
+
+
+def gelu_parts(gate):
+    slope = 0.7978845608
+    bend = 0.044715
+    square = gate * gate
+    tanh = jnp.tanh(slope * gate * (1.0 + bend * square))
+    half = 0.5 * (1.0 + tanh)
+    grad = half + 0.5 * slope * gate * (1.0 - tanh * tanh) * (1.0 + 3.0 * bend * square)
+    return gate * half, grad
+
+
+def experts_kernel(
+    h2_ref,
+    share_ref,
+    c_all_ref,
+    gate_up_ref,
+    down_ref,
+    h2_all_ref,
+    dgu_ref,
+    hidden_ref,
+    du_ref,
+    w_gu,
+    w_down,
+    h2_all,
+    c_all,
+    dhid,
+    gu,
+    hidden,
+    dgu,
+    du,
+    share,
+    load_sems,
+    out_sems,
+    gather_sems,
+):
+    rows = h2_ref.shape[0]
+    half = rows // 2
+    two = 2 * rows
+    dp = lax.axis_index("dp")
+    loads = [
+        pltpu.make_async_copy(down_ref.at[dp], w_down, load_sems.at[0]),
+        pltpu.make_async_copy(c_all_ref, c_all, load_sems.at[1]),
+        pltpu.make_async_copy(gate_up_ref.at[dp], w_gu, load_sems.at[2]),
+    ]
+    for load in loads:
+        load.start()
+    greet([flip("dp", 1), flip("expert", 2), flip("expert", 1)])
+    gather = GroupGather(h2_ref, h2_all, gather_sems, rows)
+    gather.start()
+    h2_all[0:rows] = h2_ref[...]
+
+    expert = lax.axis_index("expert") * lax.axis_size("dp") + dp
+    columns = []
+    for code in range(8):
+        turned = share_ref[code].T
+        mine = lax.broadcasted_iota(jnp.int32, turned.shape, 1) == expert
+        columns.append(jnp.sum(jnp.where(mine, turned, 0.0), axis=1, keepdims=True))
+    for which, codes in enumerate(SLOT_CODES):
+        for index, code in enumerate(codes):
+            part = (index % 2) * half
+            share[pl.ds(which * two + index * half, half), :] = columns[code][part : part + half]
+
+    loads[0].wait()
+    loads[1].wait()
+    for which in range(4):
+        span = slice(which * two, (which + 1) * two)
+        dhid[span] = matmul(c_all[span], w_down[...], NT)
+    loads[2].wait()
+
+    outs = []
+
+    def out(number, src, dst, span):
+        copy = pltpu.make_async_copy(src.at[span], dst.at[span], out_sems.at[number])
+        copy.start()
+        outs.append(copy)
+
+    for which in range(4):
+        span = slice(which * two, (which + 1) * two)
+        place = pl.ds(which * two, two)
+        if which > 1:
+            gather.forward(which)
+        gather.arrived(which)
+        out(4 * which, h2_all, h2_all_ref, place)
+        gu[...] = matmul(h2_all[span], w_gu[...])
+
+        def activate(step, carry):
+            near = pl.ds(pl.multiple_of(step * half, half), half)
+            far = pl.ds(pl.multiple_of(which * two + step * half, half), half)
+            up = gu[near, FF:]
+            activated, grad = gelu_parts(gu[near, :FF])
+            scale = share[far, :]
+            upstream = dhid[far, :] * scale
+            hidden[far, :] = (activated * up * scale).astype(BF)
+            dgu[far, :FF] = (upstream * up * grad).astype(BF)
+            dgu[far, FF:] = (upstream * activated).astype(BF)
+            return carry
+
+        lax.fori_loop(0, 4, activate, 0)
+        if which == 0:
+            gather.forward(1)
+        out(4 * which + 1, dgu, dgu_ref, place)
+        out(4 * which + 2, hidden, hidden_ref, place)
+        du[span] = matmul(dgu[span], w_gu[...], NT).astype(BF)
+        out(4 * which + 3, du, du_ref, place)
+    gather.finish()
+    for copy in outs:
+        copy.wait()
+
+
+def experts(h2, share_all, c_all, gate_up, down):
+    rows = h2.shape[0]
+    total = 8 * rows
+    shape = jax.ShapeDtypeStruct
+    return pl.pallas_call(
+        experts_kernel,
+        out_shape=[
+            shape((total, D), BF),
+            shape((total, 2 * FF), BF),
+            shape((total, FF), BF),
+            shape((total, D), BF),
+        ],
+        in_specs=[VM] * 2 + [ANY] * 3,
+        out_specs=[ANY] * 4,
+        scratch_shapes=[
+            pltpu.VMEM(gate_up.shape[1:], BF),
+            pltpu.VMEM(down.shape[1:], BF),
+            pltpu.VMEM((total, D), BF),
+            pltpu.VMEM((total, D), BF),
+            pltpu.VMEM((total, FF), F32),
+            pltpu.VMEM((2 * rows, 2 * FF), F32),
+            pltpu.VMEM((total, FF), BF),
+            pltpu.VMEM((total, 2 * FF), BF),
+            pltpu.VMEM((total, D), BF),
+            pltpu.VMEM((total, 1), F32),
+            pltpu.SemaphoreType.DMA((3,)),
+            pltpu.SemaphoreType.DMA((16,)),
+            GATHER_SEMS,
+        ],
+        compiler_params=pltpu.CompilerParams(
+            collective_id=1, has_side_effects=True, vmem_limit_bytes=60 << 20
+        ),
+        cost_estimate=pl.CostEstimate(
+            flops=2 * total * D * FF * 5, bytes_accessed=50 << 20, transcendentals=total * FF
+        ),
+    )(h2, share_all, c_all, gate_up, down)
+
+
+def fast_body(
+    packed_in,
+    routes,
+    gates,
+    doc_starts,
+    attn_gain,
+    w_qkv,
+    w_out,
+    ffn_gain,
+    expert_gate_up,
+    expert_down,
+    cotangent,
+):
+    tokens = packed_in[0].astype(F32)
+    rows = tokens.shape[0]
+    heads = QUERY_HEADS // KEY_VALUE_HEADS
+    query_width = QUERY_HEADS * HEAD_SIZE
+    key_value_width = KEY_VALUE_HEADS * HEAD_SIZE
+    scaling = HEAD_SIZE ** (-0.5)
+    contexts = lax.axis_size("context")
+    dp = lax.axis_index("dp")
+    own = dp * lax.axis_size("expert") + lax.axis_index("expert")
+    begins, cosine, sine, share = prepare(routes, gates, doc_starts, rows, 8)
+    (h1, query, att, logsum, merged, residual, h2, kv, c_all, share_all) = attention_forward(
+        packed_in[0],
+        share,
+        begins,
+        cosine,
+        sine,
+        attn_gain[None],
+        ffn_gain[None],
+        cotangent[0],
+        w_qkv,
+        w_out,
+    )
+    h2_all, dgu, hidden, du = experts(h2, share_all, c_all, expert_gate_up, expert_down)
+    down_grad = matmul(hidden, c_all, TN)
+    gate_up_grad = matmul(h2_all, dgu, TN)
+    y = matmul(hidden, lax.dynamic_index_in_dim(expert_down, dp, 0, False)).astype(BF)
+
+    def home(values):
+        half = rows // 2
+        parts = values.reshape(16, half, D)
+        halves = {}
+        for which, codes in enumerate(SLOT_CODES):
+            for index, code in enumerate(codes):
+                halves[code, index % 2] = parts[4 * which + index]
+        stacked = jnp.stack(
+            [jnp.concatenate([halves[code, 0], halves[code, 1]]) for code in range(8)]
+        )
+        placed = stacked[jnp.arange(8) ^ own].reshape(8 * rows, D)
+        return lax.psum_scatter(placed, ("dp", "expert"), scatter_dimension=0, tiled=True)
+
+    packed_out = (residual + home(y).astype(F32)).astype(BF)
+    upstream = cotangent[0].astype(F32)
+    inverse_f = lax.rsqrt(jnp.mean(residual * residual, axis=-1, keepdims=True) + epsilon)
+    grad_part, ffn_gain_grad = norm_back(residual, inverse_f, ffn_gain, home(du).astype(F32))
+    grad_residual = upstream + grad_part
+    grad_branch = grad_residual.astype(BF)
+    out_proj_grad = matmul(merged, grad_branch, TN)
+    merged_gradient = matmul(grad_branch, w_out, NT).astype(BF)
+    output_gradient = jnp.transpose(
+        merged_gradient.reshape(rows, KEY_VALUE_HEADS, heads, HEAD_SIZE), (1, 2, 0, 3)
+    )
+    att = jnp.transpose(att, (0, 2, 1)).reshape(KEY_VALUE_HEADS, heads, rows, HEAD_SIZE)
+    delta = jnp.sum(output_gradient.astype(F32) * att, axis=-1)
+    logsum = logsum[:QUERY_HEADS].reshape(KEY_VALUE_HEADS, heads, rows)
+    query = jnp.transpose(
+        query.reshape(KEY_VALUE_HEADS, heads, rows, HEAD_SIZE), (2, 0, 1, 3)
+    )
+    known = jnp.arange(contexts) <= lax.axis_index("context")
+    kv = jnp.where(known[:, None, None], kv, 0).reshape(contexts * rows, -1)
+    keys = kv[:, :key_value_width].reshape(-1, KEY_VALUE_HEADS, HEAD_SIZE)
+    values = kv[:, key_value_width:].reshape(-1, KEY_VALUE_HEADS, HEAD_SIZE)
+    positions = lax.axis_index("context") * rows + jnp.arange(rows, dtype=jnp.int32)
+    grad_query, grad_key, grad_value = attend_back(
+        query,
+        output_gradient,
+        logsum,
+        delta,
+        positions,
+        begins[0],
+        keys,
+        values,
+        0,
+        scaling,
+    )
+    both = jnp.concatenate([grad_key, grad_value], axis=1).astype(BF)
+    both = lax.psum_scatter(both, "context", scatter_dimension=0, tiled=True).astype(F32)
+    half_cos, half_sin = cosine[:, : HEAD_SIZE // 2], sine[:, HEAD_SIZE // 2 :]
+    grad_q_rows = apply_rotary(
+        jnp.transpose(grad_query, (2, 0, 1, 3)).reshape(rows, QUERY_HEADS, HEAD_SIZE),
+        half_cos,
+        half_sin,
+        False,
+    )
+    grad_k_rows = apply_rotary(both[:, :KEY_VALUE_HEADS], half_cos, half_sin, False)
+    grad_projected = jnp.concatenate(
+        [
+            grad_q_rows.reshape(rows, query_width),
+            grad_k_rows.reshape(rows, key_value_width),
+            both[:, KEY_VALUE_HEADS:].reshape(rows, key_value_width),
+        ],
+        axis=-1,
+    ).astype(BF)
+    qkv_grad = matmul(h1, grad_projected, TN)
+    inverse_a = lax.rsqrt(jnp.mean(tokens * tokens, axis=-1, keepdims=True) + epsilon)
+    grad_part, attn_gain_grad = norm_back(
+        tokens, inverse_a, attn_gain, matmul(grad_projected, w_qkv, NT)
+    )
+    packed_grad = grad_residual + grad_part
+
+    def scattered(values, axes):
+        part = lax.psum_scatter(values.astype(BF), "context", scatter_dimension=0, tiled=True)
+        return part if axes is None else lax.psum(part, axes).astype(F32)
+
+    dense = ("dp", "expert")
+    gate_up_own, down_own = scattered(gate_up_grad, None), scattered(down_grad, None)
+    gate_up_both = lax.all_gather(gate_up_own, "dp", axis=0).astype(F32)
+    down_both = lax.all_gather(down_own, "dp", axis=0).astype(F32)
+    return (
+        packed_out[None],
+        packed_grad[None],
+        scattered(attn_gain_grad, dense),
+        scattered(qkv_grad, dense),
+        scattered(out_proj_grad, dense),
+        scattered(ffn_gain_grad, dense),
+        gate_up_both,
+        down_both,
+    )
+
+
+def fits(mesh):
+    sizes = mesh.shape
+    contexts = sizes["context"]
+    return (
+        sizes["dp"] == 2
+        and sizes["expert"] == 4
+        and D % (contexts * 128) == 0
+        and FF % (contexts * 64) == 0
+    )
+
+
 def solution(mesh):
+    chosen_body = fast_body if fits(mesh) else body
     placed = (
         P(("dp", "expert"), "context", None),
         P(("dp", "expert"), "context", None),
@@ -425,7 +1078,7 @@
         P(("dp", "expert"), "context", None),
     )
     return jax.shard_map(
-        body,
+        chosen_body,
         mesh=mesh,
         in_specs=placed,
         out_specs=(

time: 1130 us -> 782 us (0.69)
  waiting for transfers between devices: 727 us -> 491 us
  Pallas kernels: 0 us -> 91.7 us
  local copies, waits for them, and re-layouts: 118 us -> 39 us
  matrix products: 119 us -> 79.2 us
  blocking collectives: 58.4 us -> 23.2 us
  starting transfers between devices: 21.1 us -> 1.2 us
  other arithmetic: 58.6 us -> 39.6 us
    all_to_all x4 -> x0, waiting for transfers between devices: 133 us -> none  [the longest x1 39.8 us: body(): lax.all_to_all(produced.astype(jnp.bfloat16), 'expert', split_axis=0, con...]
    pallas_call x0 -> x2, Pallas kernels: none -> 91.7 us  [the longest x1 46.3 us: experts(): pl.pallas_call(experts_kernel, out_shape=[shape((total, D), BF), shape((t...]
    reduce_scatter x6 -> x7, waiting for transfers between devices: 466 us -> 398 us  [the longest x4 286 us: scattered(): lax.psum_scatter(values.astype(BF), 'context', scatter_dimension=0, tiled...]
    psum x2 -> x1, waiting for transfers between devices: 127 us -> 65 us  [scattered(): return part if axes is None else lax.psum(part, axes).astype(F32)]
    dot_general x14 -> x7, matrix products: 110 us -> 52.5 us  [matmul(): return lax.dot_general(left, right, dims, preferred_element_type=F32)]
    all_gather x2 -> x0, blocking collectives: 35.2 us -> none  [the longest x1 18 us: body(): part_keys = lax.all_gather(key_matrix, 'context', axis=0, tiled=True)]
    gather x2, local copies, waits for them, and re-layouts: 46.5 us -> 13.1 us  [home(): placed = stacked[jnp.arange(8) ^ own].reshape(8 * rows, D)]
    all_gather x0 -> x2, waiting for transfers between devices: none -> 27.8 us  [the longest x1 23 us: fast_body(): down_both = lax.all_gather(down_own, 'dp', axis=0).astype(F32)]
  transfers between devices with their start and end apart: 12 -> 10, of which waited for: 12 -> 10; matrix products, arithmetic and copies ran while one was open for 12% -> 16% of each run, Pallas kernels for 0% -> 0%
where the time goes in v1:
time: 782 us; the launch traced here: 780 us
  waiting for transfers between devices  491 us (63%)
  Pallas kernels  91.7 us (12%)
  matrix products  79.2 us (10%)
  other arithmetic  39.6 us (5%)
  local copies, waits for them, and re-layouts  39 us (5%)
  blocking collectives  23.2 us (3%)
  between operations  15.4 us (2%)
    reduce_scatter x4, waiting for transfers between devices, scattered(): lax.psum_scatter(values.astype(BF), 'context', scatter_dimension=0, tiled...  286 us
    reduce_scatter x2, waiting for transfers between devices, home(): lax.psum_scatter(placed, ('dp', 'expert'), scatter_dimension=0, tiled=True)  91.4 us
    psum x1, waiting for transfers between devices, scattered(): return part if axes is None else lax.psum(part, axes).astype(F32)  65 us
    dot_general x7, matrix products, matmul(): return lax.dot_general(left, right, dims, preferred_element_type=F32)  52.5 us
    pallas_call x1, Pallas kernels, experts(): pl.pallas_call(experts_kernel, out_shape=[shape((total, D), BF), shape((t...  46.3 us
    pallas_call x1, Pallas kernels, attention_forward(): pl.pallas_call(attention_kernel, out_shape=[shape((rows, D), BF), shape((...  45.5 us
    all_gather x1, waiting for transfers between devices, fast_body(): down_both = lax.all_gather(down_own, 'dp', axis=0).astype(F32)  23 us
    reduce_scatter x1, waiting for transfers between devices, fast_body(): lax.psum_scatter(both, 'context', scatter_dimension=0, tiled=True)  20.5 us
  transfers between devices with their start and end apart: 10, of which 10 were waited for; matrix products, arithmetic and copies ran while one was open for 16% of the time, Pallas kernels for 0%

profile of v1, /device:TPU:0, one launch (start us, length us, event | category | flops | bytes accessed | tf_op | source)
XLA Modules:
  0.0 779.9 jit_solution(9994638581896647730)
XLA Ops:
  8.0 1.3 broadcast_in_dim.85.attn_gain_ref
  9.3 1.3 broadcast_in_dim.86.ffn_gain_ref
  10.6 1.3 select_reduce_fusion.share_ref
  13.3 45.5 %shard_map.170 = (bf16[256,1536]{1,0:T(8,128)(2,1)}, bf16[12,256,128]{2,1,0:T(8,128)(2,1)}, f32[12,128,256]{2,1,0:T(8,128)}, f32[16,256]{1,0:T(8,128)}, bf16[256...) custom-call(bf16[256,1536]{1,0:T(8,128)(2,1)} %bitcast.172, ...), custom_call_target="tpu_custom_call" | custom-call | flops 3221225472 | bytes 31457280 | tf_op jit(solution)/shard_map/pallas_call | solution.py:724
  58.8 46.3 %shard_map.171 = (bf16[2048,1536]{1,0:T(8,128)(2,1)}, bf16[2048,1536]{1,0:T(8,128)(2,1)}, bf16[2048,768]{1,0:T(8,128)(2,1)}, bf16[2048,1536]{1,0:T(8,128)(2,1)}) custom-call(bf16[256,1536]{1,0:T(8,128)(2,1)} %get-tuple-element.23.h2_ref, f32[8,8,256]{2,1,0:T(8,128)} %get-tuple-element.24.share_ref, bf16[2048,1536]{1,0:T(8,128)(2,1)} %get-tuple-element.25.c_all_ref, ...), custom_call_target="tpu_custom_call" | custom-call | flops 24159191040 | bytes 52428800 | tf_op jit(solution)/shard_map/pallas_call | solution.py:888
  105.0 2.1 bitcast_dynamic-update-slice_fusion.3
  107.1 2.1 fusion.62
  109.3 2.1 bitcast_dynamic-update-slice_fusion.2
  115.1 2.1 bitcast_dynamic-update-slice_fusion.1
  117.2 2.1 bitcast_dynamic-update-slice_fusion
  119.3 6.4 gather_fusion.1
  125.8 7.4 convolution_convert_fusion.1
  141.2 6.6 gather_fusion
  147.9 10.2 %convolution_convert_fusion.4 = bf16[768,1536]{1,0:T(8,128)(2,1)} fusion(bf16[2048,768]{1,0:T(8,128)(2,1)} %get-tuple-element.26, bf16[2048,1536]{1,0:T(8,128)(2,1)} %get-tuple-element.25.c_all_ref), kind=kOutput, calls=%fused_computation.13 | convolution fusion | flops 4833017856 | bytes 11796480 | tf_op jit(solution)/shard_map/dot_general | solution.py:424
  159.7 1.4 broadcast_select_fusion
  162.1 1.4 copy.120
  163.6 2.2 copy.121
  165.8 1.2 copy.88
  167.0 6.4 fusion.65
  173.4 27.5 %reduce-scatter.10.cloned.1.call-done = bf16[256,1536]{1,0:T(8,128)(2,1)} async-done(((bf16[2048,1536]{1,0:T(8,128)(2,1)}), bf16[256,1536]{1,0:T(8,128)(2,1)}) %reduce-scatter.10.cloned.1.call-update) | async-done | bytes 786448 | tf_op jit(solution)/shard_map/reduce_scatter | solution.py:973
  200.9 1.6 fusion.14
  202.5 63.9 %reduce-scatter.8.cloned.1.call-done = bf16[256,1536]{1,0:T(8,128)(2,1)} async-done(((bf16[2048,1536]{1,0:T(8,128)(2,1)}), bf16[256,1536]{1,0:T(8,128)(2,1)}) %reduce-scatter.8.cloned.1.call-update) | async-done | bytes 786448 | tf_op jit(solution)/shard_map/reduce_scatter | solution.py:973
  266.4 3.2 fusion.11
  269.5 3.7 convolution_convert_fusion.5
  273.6 1.6 multiply_reduce_fusion
  275.2 7.1 multiply_convert_fusion
  282.3 2.2 fusion.36
  284.4 7.3 fusion.33
  293.1 15.6 %convolution_convert_fusion.3 = bf16[1536,1536]{1,0:T(8,128)(2,1)} fusion(bf16[2048,1536]{1,0:T(8,128)(2,1)} %get-tuple-element.34, bf16[2048,1536]{1,0:T(8,128)(2,1)} %get-tuple-element.35), kind=kOutput, calls=%fused_computation.10 | convolution fusion | flops 9666035712 | bytes 17301504 | tf_op jit(solution)/shard_map/dot_general | solution.py:424
  308.8 8.5 %reduce-scatter.20.cloned.1.call-done = bf16[192,1536]{1,0:T(8,128)(2,1)} async-done(((bf16[768,1536]{1,0:T(8,128)(2,1)}), bf16[192,1536]{1,0:T(8,128)(2,1)}) %reduce-scatter.20.cloned.1.call-update) | async-done | bytes 589840 | tf_op jit(solution)/shard_map/reduce_scatter | solution.py:1035
  317.4 3.6 convolution_convert_fusion.2
  322.1 3.8 convolution_multiply_fusion
  326.2 20.5 %reduce-scatter.12.cloned.1.call-done = bf16[256,4,128]{0,2,1:T(8,128)(2,1)} async-done(((bf16[1024,4,128]{0,2,1:T(8,128)(2,1)}), bf16[256,4,128]{0,2,1:T(8,128)(2,1)}) %reduce-scatter.12.cloned.1.call-update) | async-done | bytes 262160 | tf_op jit(solution)/shard_map/reduce_scatter | solution.py:1010
  348.7 6.0 convolution_convert_fusion
  354.7 78.2 %reduce-scatter.18.cloned.1.call-done = bf16[384,1536]{1,0:T(8,128)(2,1)} async-done(((bf16[1536,1536]{1,0:T(8,128)(2,1)}), bf16[384,1536]{1,0:T(8,128)(2,1)}) %reduce-scatter.18.cloned.1.call-update) | async-done | bytes 1179664 | tf_op jit(solution)/shard_map/reduce_scatter | solution.py:1035
  434.7 23.0 %all-gather.7.cloned.1.call-done = bf16[384,1536]{1,0:T(8,128)(2,1)} async-done(((bf16[192,1536]{1,0:T(8,128)(2,1)}), bf16[384,1536]{1,0:T(8,128)(2,1)}) %all-gather.7.cloned.1.call-update) | async-done | bytes 1179664 | tf_op jit(solution)/shard_map/all_gather | solution.py:1041
  457.7 3.0 convert.34
  460.7 85.3 %reduce-scatter.16.cloned.1.call-done = bf16[384,1536]{1,0:T(8,128)(2,1)} async-done(((bf16[1536,1536]{1,0:T(8,128)(2,1)}), bf16[384,1536]{1,0:T(8,128)(2,1)}) %reduce-scatter.16.cloned.1.call-update) | async-done | bytes 1179664 | tf_op jit(solution)/shard_map/reduce_scatter | solution.py:1035
  546.0 113.7 %reduce-scatter.14.cloned.1.call-done = bf16[384,2048]{1,0:T(8,128)(2,1)} async-done(((bf16[1536,2048]{1,0:T(8,128)(2,1)}), bf16[384,2048]{1,0:T(8,128)(2,1)}) %reduce-scatter.14.cloned.1.call-update) | async-done | bytes 1572880 | tf_op jit(solution)/shard_map/reduce_scatter | solution.py:1035
  659.7 5.9 fusion.24
  665.7 11.1 %all-reduce.4 = (bf16[1536]{0:T(1024)(128)(2,1)S(1)}, bf16[1536]{0:T(1024)(128)(2,1)S(1)}) all-reduce(bf16[1536]{0:T(1024)(128)(2,1)S(1)} %get-tuple-element.38, bf16[1536]{0:T(1024)(128)(2,1)S(1)} %get-tuple-element.36), channel_id=7, replica_groups=mesh['dp'=2,'context'=4,'expert'=4] {'context'}, use_global_device_ids=true, to_apply=%region_11.12.clone | all-reduce | flops 3072 | bytes 12288
  676.9 12.1 %all-reduce.2 = (bf16[384]{0:T(512)(128)(2,1)S(1)}, bf16[384]{0:T(512)(128)(2,1)S(1)}) all-reduce(bf16[384]{0:T(512)(128)(2,1)S(1)} %dynamic-slice.1, bf16[384]{0:T(512)(128)(2,1)S(1)} %dynamic-slice.3), channel_id=1, replica_groups=mesh['dp'=2,'context'=4,'expert'=4] {'dp','expert'}, use_global_device_ids=true, to_apply=%region_12.13 | all-reduce | flops 768 | bytes 3072 | tf_op jit(solution)/shard_map/psum | solution.py:1036
  690.2 3.1 fusion.21
  693.3 4.8 all-gather.5.cloned.1.call-done
  698.1 4.5 convert.33
  702.6 65.0 %all-reduce.7.cloned.1.call-done = (bf16[384,2048]{1,0:T(8,128)(2,1)}, bf16[384,1536]{1,0:T(8,128)(2,1)}) async-done(((bf16[384,2048]{1,0:T(8,128)(2,1)}, bf16[384,1536]{1,0:T(8,128)(2,1)}), (bf16[384,2048]{1,0:T(8,128)(2,1)}, bf16[384,1536]{1,0:T(8,128)(2,1)})) %all-reduce.7.cloned.1.call-update) | async-done | bytes 2752528 | tf_op jit(solution)/shard_map/psum | solution.py:1036
  767.6 3.5 convert_element_type.99
  771.1 1.7 convert_element_type.101
  (98 shorter events, 24.2 us)
Async XLA Ops:
  7.2 193.7 %reduce-scatter.10.cloned.1.call-start = ((), (), s32[]{:S(2)}) async-start(), calls=%async_computation.8 | async-start | bytes 7077888 | tf_op jit(solution)/shard_map/reduce_scatter | solution.py:973
  8.0 5.3 copy-start.12
  125.8 140.6 %reduce-scatter.8.cloned.1.call-start = ((), (), s32[]{:S(2)}) async-start(), calls=%async_computation.7 | async-start | bytes 7077888 | tf_op jit(solution)/shard_map/reduce_scatter | solution.py:973
  147.8 10.8 %copy-start.13 = (s32[256]{0:T(256)S(1)}, s32[256]{0:T(256)}, u32[]{:S(2)}) copy-start(s32[256]{0:T(256)} %copy-done.12) | copy-start | bytes 3076
  147.8 11.7 %copy-start.1 = (f32[256,1536]{1,0:T(8,128)S(1)}, f32[256,1536]{1,0:T(8,128)}, u32[]{:S(2)}) copy-start(f32[256,1536]{1,0:T(8,128)} %get-tuple-element.22) | copy-start | bytes 4718596
  147.9 169.5 %reduce-scatter.20.cloned.1.call-start = ((), (), s32[]{:S(2)}) async-start(), calls=%async_computation.13 | async-start | bytes 2949120 | tf_op jit(solution)/shard_map/reduce_scatter | solution.py:1035
  158.1 5.5 copy-start.14
  158.1 7.7 copy-start.6
  158.1 188.6 %reduce-scatter.12.cloned.1.call-start = ((), (), s32[]{:S(2)}) async-start(), calls=%async_computation.9 | async-start | bytes 1310720 | tf_op jit(solution)/shard_map/reduce_scatter | solution.py:1010
  163.5 9.8 %copy-start.3 = (bf16[1024,256]{0,1:T(8,128)(2,1)}, bf16[1024,256]{0,1:T(8,128)(2,1)S(1)}, u32[]{:S(2)}) copy-start(bf16[1024,256]{0,1:T(8,128)(2,1)S(1)} %copy.120) | copy-start | bytes 1572868
  167.0 33.9 %copy-start.10 = (f32[1536]{0:T(1024)S(1)}, f32[1536]{0:T(1024)}, u32[]{:S(2)}) copy-start(f32[1536]{0:T(1024)} %param.18) | copy-start | bytes 18436
  275.2 7.1 copy-start.5
  282.2 9.5 %copy-start = (bf16[2,6,256,1024]{2,3,1,0:T(8,128)(2,1)}, bf16[2,6,256,1024]{2,3,1,0:T(8,128)(2,1)S(1)}, u32[]{:S(2)}) copy-start(bf16[2,6,256,1024]{2,3,1,0:T(8,128)(2,1)S(1)} %multiply_convert_fusion) | copy-start | bytes 18874372
  282.3 2.2 copy-start.9
  292.9 140.0 %reduce-scatter.18.cloned.1.call-start = ((), (), s32[]{:S(2)}) async-start(), calls=%async_computation.12 | async-start | bytes 5898240 | tf_op jit(solution)/shard_map/reduce_scatter | solution.py:1035
  308.7 8.7 %copy-start.7 = (bf16[256,1536]{1,0:T(8,128)(2,1)S(1)}, bf16[256,1536]{1,0:T(8,128)(2,1)}, u32[]{:S(2)}) copy-start(bf16[256,1536]{1,0:T(8,128)(2,1)} %get-tuple-element.33) | copy-start | bytes 2359300
  308.8 149.0 %all-gather.7.cloned.1.call-start = ((), (), s32[]{:S(2)}) async-start(), calls=%async_computation.15 | async-start | bytes 1769472 | tf_op jit(solution)/shard_map/all_gather | solution.py:1041
  317.4 228.6 %reduce-scatter.16.cloned.1.call-start = ((), (), s32[]{:S(2)}) async-start(), calls=%async_computation.11 | async-start | bytes 5898240 | tf_op jit(solution)/shard_map/reduce_scatter | solution.py:1035
  321.0 1.0 copy-start.4
  321.1 338.6 %reduce-scatter.14.cloned.1.call-start = ((), (), s32[]{:S(2)}) async-start(), calls=%async_computation.10 | async-start | bytes 7864320 | tf_op jit(solution)/shard_map/reduce_scatter | solution.py:1035
  354.6 78.6 %copy-start.15 = (u32[32]{0:T(128)S(1)}, u32[32]{0:T(128)}, u32[]{:S(2)}) copy-start(u32[32]{0:T(128)} %constant.61) | copy-start | bytes 388
  354.6 79.8 %copy-start.2 = (bf16[1,256,1536]{2,1,0:T(8,128)(2,1)S(1)}, bf16[1,256,1536]{2,1,0:T(8,128)(2,1)}, u32[]{:S(2)}) copy-start(bf16[1,256,1536]{2,1,0:T(8,128)(2,1)} %param.11) | copy-start | bytes 2359300
  354.7 305.1 %copy-start.11 = (f32[1536]{0:T(1024)S(1)}, f32[1536]{0:T(1024)}, u32[]{:S(2)}) copy-start(f32[1536]{0:T(1024)} %param.15) | copy-start | bytes 18436
  354.7 343.4 %all-gather.5.cloned.1.call-start = ((), (), s32[]{:S(2)}) async-start(), calls=%async_computation.14 | async-start | bytes 3538944 | tf_op jit(solution)/shard_map/all_gather | solution.py:1040
  432.9 334.6 %all-reduce.7.cloned.1.call-start = ((), (), s32[]{:S(2)}) async-start(), calls=%async_computation.16 | async-start | bytes 5505024 | tf_op jit(solution)/shard_map/psum | solution.py:1036
  767.6 3.5 copy-start.8
Sparse Core Ops, SparseCore 0:
  125.9 74.9 reduce-scatter.9
  204.6 61.7 reduce-scatter.7
  269.3 48.0 reduce-scatter.19
  320.1 26.5 reduce-scatter.11
  349.0 83.9 reduce-scatter.17
  434.4 23.2 all-gather.6
  460.7 85.2 reduce-scatter.15
  548.4 111.2 reduce-scatter.13
  661.3 36.6 all-gather.4
  701.6 65.9 all-reduce.6

commit v2 on v1

--- a/solution.py
+++ b/solution.py
@@ -919,6 +919,891 @@
     )(h2, share_all, c_all, gate_up, down)
 
 
+class GroupReturn:
+    def __init__(self, source, own, near, second, third, sems, rows):
+        self.rows, self.half = rows, rows // 2
+        self.own, self.near, self.second, self.third = own, near, second, third
+        x, y, core = flip("dp", 1), flip("expert", 2), flip("expert", 1)
+
+        def link(number, src, dst, peer):
+            return remote(src, dst, sems.at[0, number], sems.at[1, number], peer)
+
+        def part(which, index):
+            return own.at[which, pl.ds(index * self.half, self.half)]
+
+        self.loads = []
+        self.cores = []
+        for which in range(4):
+            begin = which * 2 * rows
+            self.loads.append(
+                pltpu.make_async_copy(
+                    source.at[pl.ds(begin, rows)], own.at[which], sems.at[0, 10 + which]
+                )
+            )
+            self.cores.append(
+                link(6 + which, source.at[pl.ds(begin + rows, rows)], near.at[which], core)
+            )
+        self.links = [
+            link(0, part(1, 0), third.at[0], x),
+            link(1, part(1, 1), third.at[1], y),
+            link(2, part(2, 0), third.at[2], y),
+            link(3, part(2, 1), third.at[3], x),
+            link(4, part(3, 0), second.at[0], y),
+            link(5, part(3, 1), second.at[1], x),
+        ]
+
+    def start(self):
+        for which in (3, 2, 1, 0):
+            self.cores[which].start()
+            self.loads[which].start()
+
+    def fold(self, which, more=()):
+        self.loads[which].wait()
+        self.cores[which].wait_recv()
+        for index in range(2):
+            span = slice(index * self.half, (index + 1) * self.half)
+            value = self.own[which, span].astype(F32) + self.near[which, span].astype(F32)
+            for extra in more:
+                value = value + extra[index].astype(F32)
+            self.own[which, span] = value.astype(BF)
+
+    def far(self):
+        self.fold(3)
+        for link in self.links[4:]:
+            link.start()
+        self.fold(2)
+        for link in self.links[2:4]:
+            link.start()
+
+    def middle(self):
+        for link in self.links[4:]:
+            link.wait_recv()
+        self.fold(1, (self.second,))
+        for link in self.links[:2]:
+            link.start()
+
+    def total(self, index):
+        span = slice(index * self.half, (index + 1) * self.half)
+        value = self.own[0, span].astype(F32) + self.near[0, span].astype(F32)
+        return value + self.third[index].astype(F32) + self.third[2 + index].astype(F32)
+
+    def settle(self):
+        self.loads[0].wait()
+        self.cores[0].wait_recv()
+        for link in self.links[:4]:
+            link.wait_recv()
+        for link in self.links + self.cores:
+            link.wait_send()
+
+    @staticmethod
+    def scratch(rows):
+        return [
+            pltpu.VMEM((4, rows, D), BF),
+            pltpu.VMEM((4, rows, D), BF),
+            pltpu.VMEM((2, rows // 2, D), BF),
+            pltpu.VMEM((4, rows // 2, D), BF),
+            pltpu.SemaphoreType.DMA((2, 14)),
+        ]
+
+
+def turned(axis, code):
+    index = lax.axis_index(axis)
+    bit = 1
+    while bit <= code:
+        if code & bit:
+            index = index + bit - 2 * bit * ((index // bit) % 2)
+        bit *= 2
+    return index
+
+
+def weights_kernel(
+    h2_all_ref,
+    dgu_ref,
+    hidden_ref,
+    c_all_ref,
+    du_ref,
+    down_ref,
+    dh2_ref,
+    gu_part_ref,
+    down_part_ref,
+    gu_in_ref,
+    down_in_ref,
+    y_ref,
+    h2_all,
+    dgu,
+    hidden,
+    c_all,
+    w_down,
+    gu_part,
+    down_part,
+    y,
+    load_sems,
+    out_sems,
+    z_sems,
+    own,
+    near,
+    second,
+    third,
+    return_sems,
+):
+    rows = dh2_ref.shape[0]
+    slice_rows = gu_part.shape[1]
+    down_rows = down_part.shape[1] // 2
+    loads = [
+        pltpu.make_async_copy(h2_all_ref, h2_all, load_sems.at[0]),
+        pltpu.make_async_copy(dgu_ref, dgu, load_sems.at[1]),
+        pltpu.make_async_copy(hidden_ref, hidden, load_sems.at[2]),
+        pltpu.make_async_copy(c_all_ref, c_all, load_sems.at[3]),
+        pltpu.make_async_copy(down_ref.at[lax.axis_index("dp")], w_down, load_sems.at[4]),
+    ]
+    for load in loads:
+        load.start()
+    z = flip("context", 1)
+    greet([flip("dp", 1), flip("expert", 2), flip("expert", 1), z])
+    back = GroupReturn(du_ref, own, near, second, third, return_sems, rows)
+    back.start()
+    outs = []
+
+    def out(number, src, dst):
+        copy = pltpu.make_async_copy(src, dst, out_sems.at[number])
+        copy.start()
+        outs.append(copy)
+
+    def gate_up_slice(code):
+        lanes = pl.ds(pl.multiple_of(turned("context", code) * slice_rows, 128), slice_rows)
+        gu_part[code] = matmul(h2_all[:, lanes], dgu[...], TN).astype(BF)
+
+    def down_pair(pair):
+        first = turned("context", 2 * pair) // 2
+        lanes = pl.ds(pl.multiple_of(first * 2 * down_rows, 128), 2 * down_rows)
+        down_part[pair] = matmul(hidden[:, lanes], c_all[...], TN).astype(BF)
+
+    loads[0].wait()
+    loads[1].wait()
+    gate_up_slice(3)
+    sends = [remote(gu_part.at[3], gu_in_ref, z_sems.at[0, 0], z_sems.at[1, 0], z)]
+    sends[0].start()
+    loads[2].wait()
+    loads[3].wait()
+    down_pair(1)
+    back.far()
+    place = pl.ds(
+        pl.multiple_of(lax.rem(turned("context", 3), 2) * down_rows, 16), down_rows
+    )
+    sends.append(
+        remote(down_part.at[1, place], down_in_ref, z_sems.at[0, 1], z_sems.at[1, 1], z)
+    )
+    sends[1].start()
+    gate_up_slice(1)
+    out(0, gu_part.at[1], gu_part_ref.at[1])
+    down_pair(0)
+    out(1, down_part, down_part_ref)
+    back.middle()
+    gate_up_slice(2)
+    out(2, gu_part.at[2], gu_part_ref.at[2])
+    gate_up_slice(0)
+    out(3, gu_part.at[0], gu_part_ref.at[0])
+    loads[4].wait()
+    for which in range(4):
+        span = pl.ds(which * 2 * rows, 2 * rows)
+        y[span] = matmul(hidden[span], w_down[...]).astype(BF)
+        out(4 + which, y.at[span], y_ref.at[span])
+    back.settle()
+    for index in range(2):
+        dh2_ref[index * rows // 2 : (index + 1) * rows // 2] = back.total(index)
+    for copy in outs + sends:
+        copy.wait()
+
+
+def expert_weights(h2_all, dgu, hidden, c_all, du, down):
+    total = h2_all.shape[0]
+    rows = total // 8
+    contexts = lax.axis_size("context")
+    slice_rows, down_rows = D // contexts, FF // contexts
+    shape = jax.ShapeDtypeStruct
+    gu_shape, down_shape = (contexts, slice_rows, 2 * FF), (contexts // 2, 2 * down_rows, D)
+    return pl.pallas_call(
+        weights_kernel,
+        out_shape=[
+            shape((rows, D), F32),
+            shape(gu_shape, BF),
+            shape(down_shape, BF),
+            shape(gu_shape[1:], BF),
+            shape((down_rows, D), BF),
+            shape((total, D), BF),
+        ],
+        in_specs=[ANY] * 6,
+        out_specs=[VM] + [ANY] * 5,
+        scratch_shapes=[
+            pltpu.VMEM((total, D), BF),
+            pltpu.VMEM((total, 2 * FF), BF),
+            pltpu.VMEM((total, FF), BF),
+            pltpu.VMEM((total, D), BF),
+            pltpu.VMEM(down.shape[1:], BF),
+            pltpu.VMEM(gu_shape, BF),
+            pltpu.VMEM(down_shape, BF),
+            pltpu.VMEM((total, D), BF),
+            pltpu.SemaphoreType.DMA((5,)),
+            pltpu.SemaphoreType.DMA((8,)),
+            pltpu.SemaphoreType.DMA((2, 2)),
+        ]
+        + GroupReturn.scratch(rows),
+        compiler_params=pltpu.CompilerParams(
+            collective_id=2, has_side_effects=True, vmem_limit_bytes=60 << 20
+        ),
+        cost_estimate=pl.CostEstimate(
+            flops=2 * total * D * FF * 4, bytes_accessed=50 << 20, transcendentals=0
+        ),
+    )(h2_all, dgu, hidden, c_all, du, down)
+
+
+def unrotate(values, cosine, sine):
+    return values * cosine - pltpu.roll(values, values.shape[1] // 2, 1) * sine
+
+
+def norm_pull(values, gain, upstream):
+    inverse = lax.rsqrt(jnp.mean(values * values, axis=-1, keepdims=True) + epsilon)
+    scaled = upstream * gain
+    inner = jnp.mean(scaled * values, axis=-1, keepdims=True)
+    grad_in = inverse * scaled - values * (inverse * inverse * inverse * inner)
+    return grad_in, jnp.sum(upstream * (values * inverse), axis=0, keepdims=True)
+
+
+def backward_kernel(
+    dh2_ref,
+    residual_ref,
+    c_ref,
+    merged_ref,
+    att_ref,
+    logsum_ref,
+    q_ref,
+    h1_ref,
+    x_ref,
+    attn_gain_ref,
+    ffn_gain_ref,
+    begin_ref,
+    cos_ref,
+    sin_ref,
+    kv_ref,
+    w_qkv_ref,
+    w_out_ref,
+    y_ref,
+    gu_part_ref,
+    down_part_ref,
+    packed_out_ref,
+    packed_grad_ref,
+    gains_ref,
+    out_proj_ref,
+    qkv_grad_ref,
+    gu_in_ref,
+    down_in_ref,
+    w_qkv,
+    w_out,
+    kv,
+    dres,
+    dbranch,
+    datt,
+    delta,
+    bias,
+    dq,
+    dkv_sum,
+    dkv_out,
+    dkv_in,
+    dqkv,
+    load_sems,
+    kv_sems,
+    z_sems,
+    dkv_sems,
+    own,
+    near,
+    second,
+    third,
+    return_sems,
+):
+    rows = x_ref.shape[0]
+    half = rows // 2
+    contexts = lax.axis_size("context")
+    me = lax.axis_index("context")
+    query_width = QUERY_HEADS * HEAD_SIZE
+    key_width = KEY_VALUE_HEADS * HEAD_SIZE
+    heads = QUERY_HEADS // KEY_VALUE_HEADS
+    scaling = HEAD_SIZE ** (-0.5)
+    down_rows = down_in_ref.shape[0]
+
+    load_out = pltpu.make_async_copy(w_out_ref, w_out, load_sems.at[0])
+    load_out.start()
+
+    def load_kv(block):
+        return pltpu.make_async_copy(kv_ref.at[block], kv.at[block], kv_sems.at[block])
+
+    def begin_load(block, carry):
+        load_kv(block).start()
+        return carry
+
+    def end_load(block, carry):
+        load_kv(block).wait()
+        return carry
+
+    lax.fori_loop(0, me + 1, begin_load, 0)
+    load_qkv = pltpu.make_async_copy(w_qkv_ref, w_qkv, load_sems.at[1])
+    load_qkv.start()
+    z = flip("context", 1)
+    greet(
+        [flip("dp", 1), flip("expert", 2), flip("expert", 1)]
+        + [other("context", step) for step in range(1, contexts)]
+    )
+    place = pl.ds(
+        pl.multiple_of(lax.rem(turned("context", 1), 2) * down_rows, 16), down_rows
+    )
+    sends = [
+        remote(gu_part_ref.at[1], gu_in_ref, z_sems.at[0, 0], z_sems.at[1, 0], z),
+        remote(down_part_ref.at[0, place], down_in_ref, z_sems.at[0, 1], z_sems.at[1, 1], z),
+    ]
+    for send in sends:
+        send.start()
+    back = GroupReturn(y_ref, own, near, second, third, return_sems, rows)
+    back.start()
+
+    grad_part, gain_grad = norm_pull(residual_ref[...], ffn_gain_ref[...], dh2_ref[...])
+    gains_ref[...] = jnp.zeros_like(gains_ref)
+    gains_ref[1:2] = gain_grad
+    dres[...] = c_ref[...].astype(F32) + grad_part
+    dbranch[...] = dres[...].astype(BF)
+    load_out.wait()
+    datt[...] = matmul(dbranch[...], w_out[...], NT).astype(BF)
+    delta[...] = jnp.zeros_like(delta)
+    for head in range(QUERY_HEADS):
+        lanes = slice(head * HEAD_SIZE, (head + 1) * HEAD_SIZE)
+        turned_grad = datt[:, lanes].astype(F32).T
+        delta[head : head + 1] = jnp.sum(turned_grad * att_ref[head], axis=0, keepdims=True)
+    back.far()
+
+    lax.fori_loop(0, me + 1, end_load, 0)
+    query_pos = me * rows + lax.broadcasted_iota(jnp.int32, (rows, rows), 1)
+    dq[...] = jnp.zeros_like(dq)
+
+    def pull(block):
+        key_pos = block * rows + lax.broadcasted_iota(jnp.int32, (rows, rows), 0)
+        allowed = (key_pos <= query_pos) & (key_pos >= begin_ref[...])
+        bias[...] = jnp.where(allowed, 0.0, negative_huge)
+        dkv_sum[...] = jnp.zeros_like(dkv_sum)
+        for head in range(QUERY_HEADS):
+            group = head // heads
+            key_lanes = slice(group * HEAD_SIZE, (group + 1) * HEAD_SIZE)
+            value_lanes = slice(key_width + group * HEAD_SIZE, key_width + (group + 1) * HEAD_SIZE)
+            keys = kv[block, :, key_lanes]
+            values = kv[block, :, value_lanes]
+            upstream = datt[:, head * HEAD_SIZE : (head + 1) * HEAD_SIZE]
+            scores = matmul(keys, q_ref[head], NT) * scaling + bias[...]
+            probs = jnp.exp(scores - logsum_ref[head : head + 1])
+            dprobs = matmul(values, upstream, NT)
+            dscores = (probs * (dprobs - delta[head : head + 1])).astype(BF)
+            dkv_sum[:, value_lanes] += matmul(probs.astype(BF), upstream)
+            dkv_sum[:, key_lanes] += matmul(dscores, q_ref[head])
+            dq[head] += matmul(keys, dscores, TN)
+
+    def dkv_copy(step):
+        return remote(
+            dkv_out.at[step],
+            dkv_in.at[step],
+            dkv_sems.at[0, step],
+            dkv_sems.at[1, step],
+            {"context": lax.rem(me - step + contexts, contexts)},
+        )
+
+    def earlier(turn, carry):
+        step = me - turn
+        pull(turn)
+        dkv_out[step] = dkv_sum[...].astype(BF)
+        dkv_copy(step).start()
+        return carry
+
+    lax.fori_loop(0, me, earlier, 0)
+    pull(me)
+    back.middle()
+
+    for head in range(QUERY_HEADS):
+        lanes = slice(head * HEAD_SIZE, (head + 1) * HEAD_SIZE)
+        dqkv[:, lanes] = unrotate(dq[head].T * scaling, cos_ref[...], sin_ref[...]).astype(BF)
+    for offset in range(0, query_width, 512):
+        lanes = slice(offset, offset + 512)
+        qkv_grad_ref[:, lanes] = matmul(h1_ref[...], dqkv[:, lanes], TN).astype(BF)
+        out_proj_ref[:, lanes] = matmul(merged_ref[...], dbranch[:, lanes], TN).astype(BF)
+
+    def later(step, carry):
+        dkv_copy(step).wait_recv()
+        dkv_sum[...] += dkv_in[step].astype(F32)
+        return carry
+
+    lax.fori_loop(1, contexts - me, later, 0)
+    for head in range(KEY_VALUE_HEADS):
+        lanes = slice(head * HEAD_SIZE, (head + 1) * HEAD_SIZE)
+        place = slice(query_width + head * HEAD_SIZE, query_width + (head + 1) * HEAD_SIZE)
+        dqkv[:, place] = unrotate(
+            dkv_sum[:, lanes] * scaling, cos_ref[...], sin_ref[...]
+        ).astype(BF)
+    dqkv[:, query_width + key_width :] = dkv_sum[:, key_width:].astype(BF)
+    qkv_grad_ref[:, query_width:] = matmul(h1_ref[...], dqkv[:, query_width:], TN).astype(BF)
+    load_qkv.wait()
+    grad_part, gain_grad = norm_pull(
+        x_ref[...].astype(F32), attn_gain_ref[...], matmul(dqkv[...], w_qkv[...], NT)
+    )
+    gains_ref[0:1] = gain_grad
+    packed_grad_ref[...] = dres[...] + grad_part
+
+    back.settle()
+    for index in range(2):
+        span = slice(index * half, (index + 1) * half)
+        packed_out_ref[span] = (residual_ref[span] + back.total(index)).astype(BF)
+
+    def sent(step, carry):
+        dkv_copy(step).wait_send()
+        return carry
+
+    lax.fori_loop(1, me + 1, sent, 0)
+    for send in sends:
+        send.wait()
+
+
+def attention_backward(
+    dh2,
+    residual,
+    cotangent,
+    merged,
+    att,
+    logsum,
+    query,
+    h1,
+    x,
+    attn_gain,
+    ffn_gain,
+    begins,
+    cosine,
+    sine,
+    kv,
+    w_qkv,
+    w_out,
+    y,
+    gu_part,
+    down_part,
+):
+    rows = x.shape[0]
+    contexts = lax.axis_size("context")
+    kv_width = 2 * KEY_VALUE_HEADS * HEAD_SIZE
+    shape = jax.ShapeDtypeStruct
+    return pl.pallas_call(
+        backward_kernel,
+        out_shape=[
+            shape((rows, D), BF),
+            shape((rows, D), F32),
+            shape((8, D), F32),
+            shape(w_out.shape, BF),
+            shape(w_qkv.shape, BF),
+            shape(gu_part.shape[1:], BF),
+            shape((down_part.shape[1] // 2, D), BF),
+        ],
+        in_specs=[VM] * 14 + [ANY] * 6,
+        out_specs=[VM] * 5 + [ANY] * 2,
+        scratch_shapes=[
+            pltpu.VMEM(w_qkv.shape, BF),
+            pltpu.VMEM(w_out.shape, BF),
+            pltpu.VMEM(kv.shape, BF),
+            pltpu.VMEM((rows, D), F32),
+            pltpu.VMEM((rows, D), BF),
+            pltpu.VMEM((rows, D), BF),
+            pltpu.VMEM(logsum.shape, F32),
+            pltpu.VMEM((rows, rows), F32),
+            pltpu.VMEM((QUERY_HEADS, HEAD_SIZE, rows), F32),
+            pltpu.VMEM((rows, kv_width), F32),
+            pltpu.VMEM((contexts, rows, kv_width), BF),
+            pltpu.VMEM((contexts, rows, kv_width), BF),
+            pltpu.VMEM((rows, w_qkv.shape[1]), BF),
+            pltpu.SemaphoreType.DMA((2,)),
+            pltpu.SemaphoreType.DMA((contexts,)),
+            pltpu.SemaphoreType.DMA((2, 2)),
+            pltpu.SemaphoreType.DMA((2, contexts)),
+        ]
+        + GroupReturn.scratch(rows),
+        compiler_params=pltpu.CompilerParams(
+            collective_id=3, has_side_effects=True, vmem_limit_bytes=60 << 20
+        ),
+        cost_estimate=pl.CostEstimate(
+            flops=2 * rows * D * 8000, bytes_accessed=40 << 20, transcendentals=rows * rows * 48
+        ),
+    )(
+        dh2,
+        residual,
+        cotangent,
+        merged,
+        att,
+        logsum,
+        query,
+        h1,
+        x,
+        attn_gain,
+        ffn_gain,
+        begins,
+        cosine,
+        sine,
+        kv,
+        w_qkv,
+        w_out,
+        y,
+        gu_part,
+        down_part,
+    )
+
+
+def bit_of(axis, bit):
+    return lax.rem(lax.axis_index(axis) // bit, 2)
+
+
+class DenseReduce:
+    def __init__(self, part, keep, near, first, second, third, fourth, out, sems):
+        self.part, self.keep, self.near, self.first = part, keep, near, first
+        self.second, self.third, self.fourth, self.out = second, third, fourth, out
+        self.sems = sems
+        self.count = 0
+        self.width = part.shape[2] // 2
+        self.rows = part.shape[1] // 8
+        self.x, self.y, self.core = flip("dp", 1), flip("expert", 2), flip("expert", 1)
+        self.xb, self.yb, self.cb = bit_of("dp", 1), bit_of("expert", 2), bit_of("expert", 1)
+        self.flows = (
+            (self.y, self.yb, self.x, self.xb),
+            (self.x, self.xb, self.y, self.yb),
+        )
+        self.pending = []
+
+    def link(self, src, dst, peer):
+        number = self.count
+        self.count += 1
+        copy = remote(src, dst, self.sems.at[0, number], self.sems.at[1, number], peer)
+        copy.start()
+        self.pending.append(copy)
+        return copy
+
+    def lanes(self, flow):
+        return slice(flow * self.width, (flow + 1) * self.width)
+
+    def span(self, bit, size, base=0):
+        return pl.ds(pl.multiple_of(base + bit * size, 16), size)
+
+    def start(self):
+        size = 4 * self.rows
+        self.load = pltpu.make_async_copy(
+            self.part.at[:, self.span(self.cb, size)], self.keep, self.sems.at[0, 16]
+        )
+        self.load.start()
+        self.copies = [
+            self.link(self.part.at[:, self.span(1 - self.cb, size)], self.near, self.core)
+        ]
+
+    def after_core(self):
+        self.load.wait()
+        self.copies[0].wait_recv()
+        slices = self.part.shape[0]
+        for index in range(slices):
+            value = self.near[index].astype(F32) + self.keep[index].astype(F32)
+            self.near[index] = value.astype(BF)
+        size = 2 * self.rows
+        self.copies = [
+            self.link(
+                self.near.at[:, self.span(1 - bit, size), self.lanes(flow)],
+                self.first.at[flow],
+                peer,
+            )
+            for flow, (peer, bit, _, _) in enumerate(self.flows)
+        ]
+
+    def after_first(self):
+        size = 2 * self.rows
+        copies = []
+        for flow, (_, bit, peer, later_bit) in enumerate(self.flows):
+            self.copies[flow].wait_recv()
+            for index in range(self.part.shape[0]):
+                value = self.near[index, self.span(bit, size), self.lanes(flow)].astype(F32)
+                value = value + self.first[flow, index].astype(F32)
+                self.first[flow, index] = value.astype(BF)
+            copies.append(
+                self.link(
+                    self.first.at[flow, :, self.span(1 - later_bit, self.rows)],
+                    self.second.at[flow],
+                    peer,
+                )
+            )
+        self.copies = copies
+
+    def after_second(self):
+        peer, bit = flip("context", 1), bit_of("context", 1)
+        copies = []
+        for flow, (_, _, _, later_bit) in enumerate(self.flows):
+            self.copies[flow].wait_recv()
+            for index in range(self.part.shape[0]):
+                value = self.first[flow, index, self.span(later_bit, self.rows)].astype(F32)
+                place = (flow, index)
+                self.second[place] = (value + self.second[place].astype(F32)).astype(BF)
+            for high in range(2):
+                copies.append(
+                    self.link(
+                        self.second.at[flow, 2 * high + 1 - bit],
+                        self.third.at[flow, high],
+                        peer,
+                    )
+                )
+        self.copies = copies
+
+    def after_third(self):
+        bit = bit_of("context", 1)
+        peer, later_bit = flip("context", 2), bit_of("context", 2)
+        copies = []
+        for flow in range(2):
+            for high in range(2):
+                self.copies[2 * flow + high].wait_recv()
+                value = self.second[flow, 2 * high + bit].astype(F32)
+                value = value + self.third[flow, high].astype(F32)
+                self.third[flow, high] = value.astype(BF)
+            copies.append(
+                self.link(self.third.at[flow, 1 - later_bit], self.fourth.at[flow], peer)
+            )
+        self.copies = copies
+
+    def place(self, flow, cuts):
+        _, bit, _, later_bit = self.flows[flow]
+        base = self.cb * 4 * self.rows + bit * 2 * self.rows
+        if cuts:
+            return pl.ds(pl.multiple_of(base, 16), 2 * self.rows)
+        return pl.ds(pl.multiple_of(base + later_bit * self.rows, 16), self.rows)
+
+    def after_fourth(self):
+        bit = bit_of("context", 2)
+        copies = []
+        for flow, (_, _, peer, _) in enumerate(self.flows):
+            self.copies[flow].wait_recv()
+            value = self.third[flow, bit].astype(F32) + self.fourth[flow].astype(F32)
+            rows, lanes = self.place(flow, 0), self.lanes(flow)
+            self.out[rows, lanes] = value.astype(BF)
+            copies.append(self.link(self.out.at[rows, lanes], self.out.at[rows, lanes], peer))
+        self.copies = copies
+
+    def spread(self):
+        copies = []
+        for flow, (peer, _, _, _) in enumerate(self.flows):
+            self.copies[flow].wait_recv()
+            rows, lanes = self.place(flow, 1), self.lanes(flow)
+            copies.append(self.link(self.out.at[rows, lanes], self.out.at[rows, lanes], peer))
+        self.copies = copies
+
+    def last(self):
+        for copy in self.copies:
+            copy.wait_recv()
+        rows = self.span(self.cb, 4 * self.rows)
+        self.copies = [self.link(self.out.at[rows], self.out.at[rows], self.core)]
+
+    def finish(self):
+        self.copies[0].wait_recv()
+        for copy in self.pending:
+            copy.wait_send()
+
+    @staticmethod
+    def scratch(contexts, rows, width):
+        quarter = rows // 8
+        return [
+            pltpu.VMEM((contexts, 4 * quarter, width), BF),
+            pltpu.VMEM((contexts, 4 * quarter, width), BF),
+            pltpu.VMEM((2, contexts, 2 * quarter, width // 2), BF),
+            pltpu.VMEM((2, contexts, quarter, width // 2), BF),
+            pltpu.VMEM((2, contexts // 2, quarter, width // 2), BF),
+            pltpu.VMEM((2, quarter, width // 2), BF),
+            pltpu.SemaphoreType.DMA((2, 17)),
+        ]
+
+
+def finish_kernel(
+    gains_ref,
+    gu_part_ref,
+    down_part_ref,
+    gu_far_ref,
+    down_far_ref,
+    gu_near_ref,
+    down_near_ref,
+    out_proj_ref,
+    qkv_grad_ref,
+    gains_out_ref,
+    out_proj_out_ref,
+    qkv_grad_out_ref,
+    weights_out_ref,
+    part,
+    arrived,
+    passed,
+    gains_in,
+    load_sems,
+    z_sems,
+    x_sems,
+    gain_sems,
+    *dense_scratch,
+):
+    slice_rows = gu_far_ref.shape[0]
+    down_rows = down_far_ref.shape[0]
+    dp = lax.axis_index("dp")
+    x, z_far = flip("dp", 1), flip("context", 2)
+
+    def down_place(code):
+        return pl.ds(
+            pl.multiple_of(lax.rem(turned("context", code), 2) * down_rows, 16), down_rows
+        )
+
+    gu_span, down_span = pl.ds(0, slice_rows), pl.ds(slice_rows, down_rows)
+    loads = []
+    for index, (code, gu_in, down_in) in enumerate(
+        ((2, gu_far_ref, down_far_ref), (0, gu_near_ref, down_near_ref))
+    ):
+        for number, (src, dst) in enumerate(
+            (
+                (gu_part_ref.at[code], part.at[index, gu_span]),
+                (down_part_ref.at[code // 2, down_place(code)], part.at[index, down_span]),
+                (gu_in, arrived.at[index, gu_span]),
+                (down_in, arrived.at[index, down_span]),
+            )
+        ):
+            loads.append(pltpu.make_async_copy(src, dst, load_sems.at[4 * index + number]))
+    for load in loads:
+        load.start()
+
+    exchange = [
+        flip("expert", 1),
+        flip("expert", 2),
+        flip("dp", 1),
+        flip("context", 1),
+        flip("context", 2),
+    ]
+    greet(exchange)
+
+    middle = len(dense_scratch) // 2
+    qkv_scratch, out_scratch = dense_scratch[:middle], dense_scratch[middle:]
+    qkv = DenseReduce(qkv_grad_ref, *qkv_scratch[:-1], qkv_grad_out_ref, qkv_scratch[-1])
+    out = DenseReduce(out_proj_ref, *out_scratch[:-1], out_proj_out_ref, out_scratch[-1])
+    dense = (out, qkv)
+    for array in dense:
+        array.start()
+
+    gains_out_ref[...] = gains_ref[...]
+    gain_copies = []
+
+    def gain_start(step):
+        copy = remote(
+            gains_out_ref,
+            gains_in.at[step],
+            gain_sems.at[0, step],
+            gain_sems.at[1, step],
+            exchange[step],
+        )
+        copy.start()
+        gain_copies.append(copy)
+
+    def gain_add(step):
+        gain_copies[step].wait()
+        gains_out_ref[...] += gains_in[step]
+
+    gain_start(0)
+    for load in loads:
+        load.wait()
+    chunk = down_rows
+    chunks = (slice_rows + down_rows) // chunk
+    z_copies, x_copies = [], []
+    for index in range(chunks):
+        span = pl.ds(index * chunk, chunk)
+        value = part[0, span].astype(F32) + arrived[0, span].astype(F32)
+        part[0, span] = value.astype(BF)
+        copy = remote(
+            part.at[0, span], passed.at[span], z_sems.at[0, index], z_sems.at[1, index], z_far
+        )
+        copy.start()
+        z_copies.append(copy)
+
+    def experts_out(index):
+        z_copies[index].wait_recv()
+        span = pl.ds(index * chunk, chunk)
+        value = part[1, span].astype(F32) + arrived[1, span].astype(F32)
+        weights_out_ref[dp, span] = (value + passed[span].astype(F32)).astype(BF)
+        copy = remote(
+            weights_out_ref.at[dp, span],
+            weights_out_ref.at[dp, span],
+            x_sems.at[0, index],
+            x_sems.at[1, index],
+            x,
+        )
+        copy.start()
+        x_copies.append(copy)
+
+    gain_add(0)
+    gain_start(1)
+    for array in dense:
+        array.after_core()
+    gain_add(1)
+    gain_start(2)
+    for array in dense:
+        array.after_first()
+    gain_add(2)
+    gain_start(3)
+    for index in range(chunks):
+        experts_out(index)
+    gain_add(3)
+    gain_start(4)
+    for array in dense:
+        array.after_second()
+    gain_add(4)
+    for array in dense:
+        array.after_third()
+    for array in dense:
+        array.after_fourth()
+    for array in dense:
+        array.spread()
+    for array in dense:
+        array.last()
+    for array in dense:
+        array.finish()
+    for copy in z_copies:
+        copy.wait_send()
+    for copy in x_copies:
+        copy.wait()
+
+
+def finish(gains, gu_part, down_part, gu_far, down_far, gu_near, down_near, out_proj, qkv_grad):
+    contexts = lax.axis_size("context")
+    slice_rows, down_rows = gu_far.shape[0], down_far.shape[0]
+    total = slice_rows + down_rows
+    shape = jax.ShapeDtypeStruct
+    out_proj = out_proj.reshape(contexts, slice_rows, -1)
+    qkv_grad = qkv_grad.reshape(contexts, slice_rows, -1)
+    return pl.pallas_call(
+        finish_kernel,
+        out_shape=[
+            shape(gains.shape, F32),
+            shape(out_proj.shape[1:], BF),
+            shape(qkv_grad.shape[1:], BF),
+            shape((2, total, D), BF),
+        ],
+        in_specs=[VM] + [ANY] * 8,
+        out_specs=[VM] * 4,
+        scratch_shapes=[
+            pltpu.VMEM((2, total, D), BF),
+            pltpu.VMEM((2, total, D), BF),
+            pltpu.VMEM((total, D), BF),
+            pltpu.VMEM((5,) + gains.shape, F32),
+            pltpu.SemaphoreType.DMA((8,)),
+            pltpu.SemaphoreType.DMA((2, total // down_rows)),
+            pltpu.SemaphoreType.DMA((2, total // down_rows)),
+            pltpu.SemaphoreType.DMA((2, 5)),
+        ]
+        + DenseReduce.scratch(contexts, slice_rows, qkv_grad.shape[2])
+        + DenseReduce.scratch(contexts, slice_rows, out_proj.shape[2]),
+        compiler_params=pltpu.CompilerParams(
+            collective_id=4, has_side_effects=True, vmem_limit_bytes=60 << 20
+        ),
+        cost_estimate=pl.CostEstimate(flops=0, bytes_accessed=40 << 20, transcendentals=0),
+    )(gains, gu_part, down_part, gu_far, down_far, gu_near, down_near, out_proj, qkv_grad)
+
+
 def fast_body(
     packed_in,
     routes,
@@ -932,122 +1817,55 @@
     expert_down,
     cotangent,
 ):
-    tokens = packed_in[0].astype(F32)
-    rows = tokens.shape[0]
-    heads = QUERY_HEADS // KEY_VALUE_HEADS
-    query_width = QUERY_HEADS * HEAD_SIZE
-    key_value_width = KEY_VALUE_HEADS * HEAD_SIZE
-    scaling = HEAD_SIZE ** (-0.5)
+    x, c = packed_in[0], cotangent[0]
+    rows = x.shape[0]
     contexts = lax.axis_size("context")
-    dp = lax.axis_index("dp")
-    own = dp * lax.axis_size("expert") + lax.axis_index("expert")
-    begins, cosine, sine, share = prepare(routes, gates, doc_starts, rows, 8)
+    expert_total = expert_gate_up.shape[0] * lax.axis_size("expert")
+    attn_gain, ffn_gain = attn_gain[None], ffn_gain[None]
+    begins, cosine, sine, share = prepare(routes, gates, doc_starts, rows, expert_total)
     (h1, query, att, logsum, merged, residual, h2, kv, c_all, share_all) = attention_forward(
-        packed_in[0],
-        share,
+        x, share, begins, cosine, sine, attn_gain, ffn_gain, c, w_qkv, w_out
+    )
+    h2_all, dgu, hidden, du = experts(h2, share_all, c_all, expert_gate_up, expert_down)
+    dh2, gu_part, down_part, gu_far, down_far, y = expert_weights(
+        h2_all, dgu, hidden, c_all, du, expert_down
+    )
+    packed_out, packed_grad, gains, out_proj, qkv_grad, gu_near, down_near = attention_backward(
+        dh2,
+        residual,
+        c,
+        merged,
+        att,
+        logsum,
+        query,
+        h1,
+        x,
+        attn_gain,
+        ffn_gain,
         begins,
         cosine,
         sine,
-        attn_gain[None],
-        ffn_gain[None],
-        cotangent[0],
+        kv,
         w_qkv,
         w_out,
-    )
-    h2_all, dgu, hidden, du = experts(h2, share_all, c_all, expert_gate_up, expert_down)
-    down_grad = matmul(hidden, c_all, TN)
-    gate_up_grad = matmul(h2_all, dgu, TN)
-    y = matmul(hidden, lax.dynamic_index_in_dim(expert_down, dp, 0, False)).astype(BF)
-
-    def home(values):
-        half = rows // 2
-        parts = values.reshape(16, half, D)
-        halves = {}
-        for which, codes in enumerate(SLOT_CODES):
-            for index, code in enumerate(codes):
-                halves[code, index % 2] = parts[4 * which + index]
-        stacked = jnp.stack(
-            [jnp.concatenate([halves[code, 0], halves[code, 1]]) for code in range(8)]
-        )
-        placed = stacked[jnp.arange(8) ^ own].reshape(8 * rows, D)
-        return lax.psum_scatter(placed, ("dp", "expert"), scatter_dimension=0, tiled=True)
-
-    packed_out = (residual + home(y).astype(F32)).astype(BF)
-    upstream = cotangent[0].astype(F32)
-    inverse_f = lax.rsqrt(jnp.mean(residual * residual, axis=-1, keepdims=True) + epsilon)
-    grad_part, ffn_gain_grad = norm_back(residual, inverse_f, ffn_gain, home(du).astype(F32))
-    grad_residual = upstream + grad_part
-    grad_branch = grad_residual.astype(BF)
-    out_proj_grad = matmul(merged, grad_branch, TN)
-    merged_gradient = matmul(grad_branch, w_out, NT).astype(BF)
-    output_gradient = jnp.transpose(
-        merged_gradient.reshape(rows, KEY_VALUE_HEADS, heads, HEAD_SIZE), (1, 2, 0, 3)
-    )
-    att = jnp.transpose(att, (0, 2, 1)).reshape(KEY_VALUE_HEADS, heads, rows, HEAD_SIZE)
-    delta = jnp.sum(output_gradient.astype(F32) * att, axis=-1)
-    logsum = logsum[:QUERY_HEADS].reshape(KEY_VALUE_HEADS, heads, rows)
-    query = jnp.transpose(
-        query.reshape(KEY_VALUE_HEADS, heads, rows, HEAD_SIZE), (2, 0, 1, 3)
-    )
-    known = jnp.arange(contexts) <= lax.axis_index("context")
-    kv = jnp.where(known[:, None, None], kv, 0).reshape(contexts * rows, -1)
-    keys = kv[:, :key_value_width].reshape(-1, KEY_VALUE_HEADS, HEAD_SIZE)
-    values = kv[:, key_value_width:].reshape(-1, KEY_VALUE_HEADS, HEAD_SIZE)
-    positions = lax.axis_index("context") * rows + jnp.arange(rows, dtype=jnp.int32)
-    grad_query, grad_key, grad_value = attend_back(
-        query,
-        output_gradient,
-        logsum,
-        delta,
-        positions,
-        begins[0],
-        keys,
-        values,
-        0,
-        scaling,
-    )
-    both = jnp.concatenate([grad_key, grad_value], axis=1).astype(BF)
-    both = lax.psum_scatter(both, "context", scatter_dimension=0, tiled=True).astype(F32)
-    half_cos, half_sin = cosine[:, : HEAD_SIZE // 2], sine[:, HEAD_SIZE // 2 :]
-    grad_q_rows = apply_rotary(
-        jnp.transpose(grad_query, (2, 0, 1, 3)).reshape(rows, QUERY_HEADS, HEAD_SIZE),
-        half_cos,
-        half_sin,
-        False,
-    )
-    grad_k_rows = apply_rotary(both[:, :KEY_VALUE_HEADS], half_cos, half_sin, False)
-    grad_projected = jnp.concatenate(
-        [
-            grad_q_rows.reshape(rows, query_width),
-            grad_k_rows.reshape(rows, key_value_width),
-            both[:, KEY_VALUE_HEADS:].reshape(rows, key_value_width),
-        ],
-        axis=-1,
-    ).astype(BF)
-    qkv_grad = matmul(h1, grad_projected, TN)
-    inverse_a = lax.rsqrt(jnp.mean(tokens * tokens, axis=-1, keepdims=True) + epsilon)
-    grad_part, attn_gain_grad = norm_back(
-        tokens, inverse_a, attn_gain, matmul(grad_projected, w_qkv, NT)
-    )
-    packed_grad = grad_residual + grad_part
-
-    def scattered(values, axes):
-        part = lax.psum_scatter(values.astype(BF), "context", scatter_dimension=0, tiled=True)
-        return part if axes is None else lax.psum(part, axes).astype(F32)
-
-    dense = ("dp", "expert")
-    gate_up_own, down_own = scattered(gate_up_grad, None), scattered(down_grad, None)
-    gate_up_both = lax.all_gather(gate_up_own, "dp", axis=0).astype(F32)
-    down_both = lax.all_gather(down_own, "dp", axis=0).astype(F32)
+        y,
+        gu_part,
+        down_part,
+    )
+    gains, out_proj, qkv_grad, weights = finish(
+        gains, gu_part, down_part, gu_far, down_far, gu_near, down_near, out_proj, qkv_grad
+    )
+    slice_rows = D // contexts
+    gains = lax.dynamic_slice_in_dim(gains, lax.axis_index("context") * slice_rows, slice_rows, 1)
     return (
         packed_out[None],
         packed_grad[None],
-        scattered(attn_gain_grad, dense),
-        scattered(qkv_grad, dense),
-        scattered(out_proj_grad, dense),
-        scattered(ffn_gain_grad, dense),
-        gate_up_both,
-        down_both,
+        gains[0],
+        qkv_grad.astype(F32),
+        out_proj.astype(F32),
+        gains[1],
+        weights[:, :slice_rows].astype(F32),
+        weights[:, slice_rows:].astype(F32),
     )
 
 
@@ -1057,6 +1875,7 @@
     return (
         sizes["dp"] == 2
         and sizes["expert"] == 4
+        and contexts == 4
         and D % (contexts * 128) == 0
         and FF % (contexts * 64) == 0
     )

time: 782 us -> 375 us (0.48)
  the two profiles are of different devices: /device:TPU:0 before, /device:TPU:27 now
where the time goes in v2:
time: 375 us; the launch traced here: 368 us
  Pallas kernels  346 us (92%)
  other arithmetic  14.8 us (4%)
  local copies, waits for them, and re-layouts  6.08 us (2%)
    pallas_call x1, Pallas kernels, finish(): pl.pallas_call(finish_kernel, out_shape=[shape(gains.shape, F32), shape(o...  132 us
    pallas_call x1, Pallas kernels, attention_backward(): pl.pallas_call(backward_kernel, out_shape=[shape((rows, D), BF), shape((r...  65.7 us
    pallas_call x1, Pallas kernels, experts(): pl.pallas_call(experts_kernel, out_shape=[shape((total, D), BF), shape((t...  54.8 us
    pallas_call x1, Pallas kernels, expert_weights(): pl.pallas_call(weights_kernel, out_shape=[shape((rows, D), F32), shape(gu...  47 us
    pallas_call x1, Pallas kernels, attention_forward(): pl.pallas_call(attention_kernel, out_shape=[shape((rows, D), BF), shape((...  45.8 us

profile of v2, /device:TPU:27, one launch (start us, length us, event | category | flops | bytes accessed | tf_op | source)
XLA Modules:
  0.0 367.6 jit_solution(3566557720018156290)
XLA Ops:
  0.6 0.7 select_reduce_fusion.1
  1.4 0.0 copy-start.4
  1.4 0.5 fusion
  2.0 0.8 pad_maximum_fusion
  2.8 1.3 broadcast_in_dim.48.attn_gain_ref
  4.1 1.3 broadcast_in_dim.49.ffn_gain_ref
  5.4 1.3 select_reduce_fusion.share_ref
  6.7 0.0 copy-done.4
  6.7 45.8 %shard_map.170 = (bf16[256,1536]{1,0:T(8,128)(2,1)}, bf16[12,256,128]{2,1,0:T(8,128)(2,1)}, f32[12,128,256]{2,1,0:T(8,128)}, f32[16,256]{1,0:T(8,128)}, bf16[256...) custom-call(bf16[256,1536]{1,0:T(8,128)(2,1)} %bitcast.12, ...), custom_call_target="tpu_custom_call" | custom-call | flops 3221225472 | bytes 31457280 | tf_op jit(solution)/shard_map/pallas_call | solution.py:724
  52.5 54.8 %shard_map.171 = (bf16[2048,1536]{1,0:T(8,128)(2,1)}, bf16[2048,1536]{1,0:T(8,128)(2,1)}, bf16[2048,768]{1,0:T(8,128)(2,1)}, bf16[2048,1536]{1,0:T(8,128)(2,1)}) custom-call(bf16[256,1536]{1,0:T(8,128)(2,1)} %get-tuple-element.39.h2_ref, f32[8,8,256]{2,1,0:T(8,128)} %get-tuple-element.40.share_ref, bf16[2048,1536]{1,0:T(8,128)(2,1)} %get-tuple-element.41.c_all_ref, ...), custom_call_target="tpu_custom_call" | custom-call | flops 24159191040 | bytes 52428800 | tf_op jit(solution)/shard_map/pallas_call | solution.py:888
  107.3 47.0 %shard_map.172 = (f32[256,1536]{1,0:T(8,128)}, bf16[4,384,1536]{2,1,0:T(8,128)(2,1)}, bf16[2,384,1536]{2,1,0:T(8,128)(2,1)}, bf16[384,1536]{1,0:T(8,128)(2,1)}, ...) custom-call(bf16[2048,1536]{1,0:T(8,128)(2,1)} %get-tuple-element.42.h2_all_ref, ...), custom_call_target="tpu_custom_call" | custom-call | flops 19327352832 | bytes 52428800 | tf_op jit(solution)/shard_map/pallas_call | solution.py:1125
  154.3 65.7 %shard_map.173 = (bf16[256,1536]{1,0:T(8,128)(2,1)}, f32[256,1536]{1,0:T(8,128)}, f32[8,1536]{1,0:T(8,128)}, bf16[1536,1536]{1,0:T(8,128)(2,1)}, bf16[1536,2048]...) custom-call(f32[256,1536]{1,0:T(8,128)} %get-tuple-element.46.dh2_ref, ...), custom_call_target="tpu_custom_call" | custom-call | flops 6291456000 | bytes 41943040 | tf_op jit(solution)/shard_map/pallas_call | solution.py:1394
  220.0 132.3 %shard_map.174 = (f32[8,1536]{1,0:T(8,128)}, bf16[384,1536]{1,0:T(8,128)(2,1)}, bf16[384,2048]{1,0:T(8,128)(2,1)}, bf16[2,576,1536]{2,1,0:T(8,128)(2,1)}) custom-call(f32[8,1536]{1,0:T(8,128)} %get-tuple-element.59.gains_ref, bf16[4,384,1536]{2,1,0:T(8,128)(2,1)} %get-tuple-element.55.gu_part_ref, bf16[2,384,1536]{2,1,0:T(8,128)(2,1)} %get-tuple-element.56.down_part_ref, ...), custom_call_target="tpu_custom_call" | custom-call | bytes 41943040 | tf_op jit(solution)/shard_map/pallas_call | solution.py:1778
  352.3 0.0 copy-start.1
  352.3 4.6 %slice_convert_fusion = f32[2,384,1536]{2,1,0:T(8,128)} fusion(bf16[2,576,1536]{2,1,0:T(8,128)(2,1)} %get-tuple-element.69), kind=kLoop, calls=%fused_computation | loop fusion | flops 1179648 | bytes 7077888 | tf_op jit(solution)/shard_map/convert_element_type | solution.py:1867
  356.9 0.0 copy-start.2
  356.9 0.0 copy-done.1
  356.9 2.0 convert_element_type.20
  358.9 0.0 copy-done.2
  358.9 0.0 copy-start.3
  358.9 0.0 copy-start
  358.9 1.7 convert_element_type.21
  360.6 3.0 slice_convert_fusion.1
  363.6 1.4 dynamic-slice_reduce_fusion
  365.1 0.0 copy-done.3
  365.1 0.9 copy.23
  365.9 0.0 copy-done
  365.9 1.1 copy.24
  (3 shorter events, 0.0 us)
Async XLA Ops:
  1.4 5.3 %copy-start.4 = (s32[256]{0:T(256)}, s32[256]{0:T(256)S(1)}, u32[]{:S(2)}) copy-start(s32[256]{0:T(256)S(1)} %select_reduce_fusion.1) | copy-start | bytes 3076
  352.3 4.6 %copy-start.1 = (bf16[384,2048]{1,0:T(8,128)(2,1)S(1)}, bf16[384,2048]{1,0:T(8,128)(2,1)}, u32[]{:S(2)}) copy-start(bf16[384,2048]{1,0:T(8,128)(2,1)} %get-tuple-element.67) | copy-start | bytes 4718596
  356.9 2.0 copy-start.2
  358.9 6.1 %copy-start.3 = (bf16[256,1536]{1,0:T(8,128)(2,1)S(1)}, bf16[256,1536]{1,0:T(8,128)(2,1)}, u32[]{:S(2)}) copy-start(bf16[256,1536]{1,0:T(8,128)(2,1)} %get-tuple-element.57) | copy-start | bytes 2359300
  358.9 7.0 %copy-start = (f32[256,1536]{1,0:T(8,128)S(1)}, f32[256,1536]{1,0:T(8,128)}, u32[]{:S(2)}) copy-start(f32[256,1536]{1,0:T(8,128)} %get-tuple-element.58) | copy-start | bytes 4718596

commit v3 on v2

--- a/solution.py
+++ b/solution.py
@@ -527,7 +527,6 @@
     w_out_ref,
     h1_ref,
     q_ref,
-    att_ref,
     logsum_ref,
     merged_ref,
     residual_ref,
@@ -678,7 +677,6 @@
     loads[2].wait()
     for head in range(QUERY_HEADS):
         attended = accumulated[head] / total[head : head + 1]
-        att_ref[head] = attended
         merged_ref[:, head * HEAD_SIZE : (head + 1) * HEAD_SIZE] = attended.T.astype(BF)
     logsum_ref[...] = jnp.where(total[...] > 0, top[...] + jnp.log(total[...]), 0.0)
     residual = x_ref[...].astype(F32) + matmul(merged_ref[...], w_out[...])
@@ -726,7 +724,6 @@
         out_shape=[
             shape((rows, D), BF),
             shape((QUERY_HEADS, rows, HEAD_SIZE), BF),
-            shape((QUERY_HEADS, HEAD_SIZE, rows), F32),
             shape((padded, rows), F32),
             shape((rows, D), BF),
             shape((rows, D), F32),
@@ -736,7 +733,7 @@
             shape((group,) + share.shape, F32),
         ],
         in_specs=[VM] * 7 + [ANY] * 3,
-        out_specs=[VM] * 7 + [ANY] * 3,
+        out_specs=[VM] * 6 + [ANY] * 3,
         scratch_shapes=[
             pltpu.VMEM(w_qkv.shape, BF),
             pltpu.VMEM(w_out.shape, BF),
@@ -929,7 +926,7 @@
             return remote(src, dst, sems.at[0, number], sems.at[1, number], peer)
 
         def part(which, index):
-            return own.at[which, pl.ds(index * self.half, self.half)]
+            return near.at[which, pl.ds(index * self.half, self.half)]
 
         self.loads = []
         self.cores = []
@@ -937,7 +934,7 @@
             begin = which * 2 * rows
             self.loads.append(
                 pltpu.make_async_copy(
-                    source.at[pl.ds(begin, rows)], own.at[which], sems.at[0, 10 + which]
+                    source.at[pl.ds(begin, rows)], own.at[which % 2], sems.at[0, 10 + which]
                 )
             )
             self.cores.append(
@@ -955,17 +952,20 @@
     def start(self):
         for which in (3, 2, 1, 0):
             self.cores[which].start()
-            self.loads[which].start()
+        self.loads[3].start()
+        self.loads[2].start()
 
     def fold(self, which, more=()):
         self.loads[which].wait()
         self.cores[which].wait_recv()
         for index in range(2):
             span = slice(index * self.half, (index + 1) * self.half)
-            value = self.own[which, span].astype(F32) + self.near[which, span].astype(F32)
+            value = self.own[which % 2, span].astype(F32) + self.near[which, span].astype(F32)
             for extra in more:
                 value = value + extra[index].astype(F32)
-            self.own[which, span] = value.astype(BF)
+            self.near[which, span] = value.astype(BF)
+        if which > 1:
+            self.loads[which - 2].start()
 
     def far(self):
         self.fold(3)
@@ -998,7 +998,7 @@
     @staticmethod
     def scratch(rows):
         return [
-            pltpu.VMEM((4, rows, D), BF),
+            pltpu.VMEM((2, rows, D), BF),
             pltpu.VMEM((4, rows, D), BF),
             pltpu.VMEM((2, rows // 2, D), BF),
             pltpu.VMEM((4, rows // 2, D), BF),
@@ -1157,6 +1157,123 @@
     )(h2_all, dgu, hidden, c_all, du, down)
 
 
+def bit_of(axis, bit):
+    return lax.rem(lax.axis_index(axis) // bit, 2)
+
+
+class DenseReduce:
+    def __init__(self, part, near, first, second, third, fourth, out, lanes, sems):
+        self.part, self.near, self.first, self.second = part, near, first, second
+        self.third, self.fourth, self.out, self.lanes = third, fourth, out, lanes
+        self.sems = sems
+        self.rows = part.shape[1] // 8
+        self.slices = part.shape[0]
+        self.x, self.y, self.core = flip("dp", 1), flip("expert", 2), flip("expert", 1)
+        self.xb, self.yb, self.cb = bit_of("dp", 1), bit_of("expert", 2), bit_of("expert", 1)
+        self.pending = []
+        self.released = 0
+
+    def send(self, src, dst, peer, amount=1):
+        number = len(self.pending)
+        copy = remote(src, dst, self.sems.at[0, number], self.sems.at[1, number], peer)
+        copy.start()
+        self.pending.append(copy)
+        self.waited = number + 1 - amount
+
+    def wait(self):
+        for copy in self.pending[self.waited :]:
+            copy.wait_recv()
+
+    def span(self, bit, size, base=0):
+        return pl.ds(pl.multiple_of(base + bit * size, 16), size)
+
+    def start(self):
+        size = 4 * self.rows
+        self.send(self.part.at[:, self.span(1 - self.cb, size)], self.near, self.core)
+
+    def release(self):
+        self.pending[0].wait_send()
+        self.released = 1
+
+    def after_core(self):
+        self.wait()
+        size = 4 * self.rows
+        for index in range(self.slices):
+            value = self.part[index, self.span(self.cb, size)].astype(F32)
+            self.near[index] = (value + self.near[index].astype(F32)).astype(BF)
+        size = 2 * self.rows
+        self.send(self.near.at[:, self.span(1 - self.yb, size)], self.first, self.y)
+
+    def after_y(self):
+        self.wait()
+        size = 2 * self.rows
+        for index in range(self.slices):
+            value = self.near[index, self.span(self.yb, size)].astype(F32)
+            self.first[index] = (value + self.first[index].astype(F32)).astype(BF)
+        self.send(self.first.at[:, self.span(1 - self.xb, self.rows)], self.second, self.x)
+
+    def after_x(self):
+        self.wait()
+        for index in range(self.slices):
+            value = self.first[index, self.span(self.xb, self.rows)].astype(F32)
+            self.second[index] = (value + self.second[index].astype(F32)).astype(BF)
+        bit = bit_of("context", 1)
+        for index in range(2):
+            source = self.second.at[2 * index + 1 - bit]
+            self.send(source, self.third.at[index], flip("context", 1), index + 1)
+
+    def after_near_z(self):
+        self.wait()
+        bit = bit_of("context", 1)
+        for index in range(2):
+            value = self.second[2 * index + bit].astype(F32) + self.third[index].astype(F32)
+            self.third[index] = value.astype(BF)
+        bit = bit_of("context", 2)
+        self.send(self.third.at[1 - bit], self.fourth, flip("context", 2))
+
+    def held(self, cuts):
+        sizes = (1, 2, 4)
+        base = self.cb * 4 * self.rows
+        if cuts < 2:
+            base = base + self.yb * 2 * self.rows
+        if cuts < 1:
+            base = base + self.xb * self.rows
+        rows = pl.ds(pl.multiple_of(base, 16), sizes[cuts] * self.rows)
+        return self.out.at[rows, self.lanes]
+
+    def after_far_z(self):
+        self.wait()
+        value = self.third[bit_of("context", 2)].astype(F32) + self.fourth[...].astype(F32)
+        place = self.held(0)
+        place[...] = value.astype(BF)
+        self.send(place, place, self.x)
+
+    def return_y(self):
+        self.wait()
+        self.send(self.held(1), self.held(1), self.y)
+
+    def return_core(self):
+        self.wait()
+        self.send(self.held(2), self.held(2), self.core)
+
+    def finish(self):
+        self.wait()
+        for copy in self.pending[self.released :]:
+            copy.wait_send()
+
+    @staticmethod
+    def scratch(contexts, rows, width):
+        least = rows // 8
+        return [
+            pltpu.VMEM((contexts, 4 * least, width), BF),
+            pltpu.VMEM((contexts, 2 * least, width), BF),
+            pltpu.VMEM((contexts, least, width), BF),
+            pltpu.VMEM((2, least, width), BF),
+            pltpu.VMEM((least, width), BF),
+            pltpu.SemaphoreType.DMA((2, 9)),
+        ]
+
+
 def unrotate(values, cosine, sine):
     return values * cosine - pltpu.roll(values, values.shape[1] // 2, 1) * sine
 
@@ -1174,7 +1291,6 @@
     residual_ref,
     c_ref,
     merged_ref,
-    att_ref,
     logsum_ref,
     q_ref,
     h1_ref,
@@ -1190,15 +1306,16 @@
     y_ref,
     gu_part_ref,
     down_part_ref,
+    gu_far_ref,
+    down_far_ref,
     packed_out_ref,
     packed_grad_ref,
     gains_ref,
     out_proj_ref,
     qkv_grad_ref,
-    gu_in_ref,
-    down_in_ref,
-    w_qkv,
-    w_out,
+    weights_ref,
+    w_dense,
+    w_kv,
     kv,
     dres,
     dbranch,
@@ -1210,28 +1327,38 @@
     dkv_out,
     dkv_in,
     dqkv,
+    dense,
+    dense_kv,
+    stage_a,
+    stage_b,
+    near_in,
+    far_in,
+    gains_in,
     load_sems,
     kv_sems,
-    z_sems,
     dkv_sems,
-    own,
-    near,
-    second,
-    third,
-    return_sems,
+    near_sems,
+    far_sems,
+    x_sems,
+    gain_sems,
+    *others,
 ):
     rows = x_ref.shape[0]
     half = rows // 2
     contexts = lax.axis_size("context")
     me = lax.axis_index("context")
+    dp = lax.axis_index("dp")
     query_width = QUERY_HEADS * HEAD_SIZE
     key_width = KEY_VALUE_HEADS * HEAD_SIZE
     heads = QUERY_HEADS // KEY_VALUE_HEADS
     scaling = HEAD_SIZE ** (-0.5)
-    down_rows = down_in_ref.shape[0]
-
-    load_out = pltpu.make_async_copy(w_out_ref, w_out, load_sems.at[0])
-    load_out.start()
+    slice_rows, down_rows = gu_far_ref.shape[0], down_far_ref.shape[0]
+    return_scratch, others = others[:5], others[5:]
+
+    def load(number, src, dst):
+        copy = pltpu.make_async_copy(src, dst, load_sems.at[number])
+        copy.start()
+        return copy
 
     def load_kv(block):
         return pltpu.make_async_copy(kv_ref.at[block], kv.at[block], kv_sems.at[block])
@@ -1244,38 +1371,89 @@
         load_kv(block).wait()
         return carry
 
+    gu_span, down_span = pl.ds(0, slice_rows), pl.ds(slice_rows, down_rows)
+
+    def down_place(code):
+        first = lax.rem(turned("context", code), 2) * down_rows
+        return down_part_ref.at[code // 2, pl.ds(pl.multiple_of(first, 16), down_rows)]
+
+    load_out = load(0, w_out_ref, w_dense)
+    stage_loads = [
+        load(2, gu_part_ref.at[2], stage_a.at[gu_span]),
+        load(3, down_place(2), stage_a.at[down_span]),
+        load(4, gu_far_ref, stage_b.at[gu_span]),
+        load(5, down_far_ref, stage_b.at[down_span]),
+    ]
     lax.fori_loop(0, me + 1, begin_load, 0)
-    load_qkv = pltpu.make_async_copy(w_qkv_ref, w_qkv, load_sems.at[1])
-    load_qkv.start()
-    z = flip("context", 1)
-    greet(
-        [flip("dp", 1), flip("expert", 2), flip("expert", 1)]
-        + [other("context", step) for step in range(1, contexts)]
-    )
-    place = pl.ds(
-        pl.multiple_of(lax.rem(turned("context", 1), 2) * down_rows, 16), down_rows
-    )
-    sends = [
-        remote(gu_part_ref.at[1], gu_in_ref, z_sems.at[0, 0], z_sems.at[1, 0], z),
-        remote(down_part_ref.at[0, place], down_in_ref, z_sems.at[0, 1], z_sems.at[1, 1], z),
-    ]
-    for send in sends:
-        send.start()
-    back = GroupReturn(y_ref, own, near, second, third, return_sems, rows)
+    load_w_kv = load(1, w_qkv_ref.at[:, query_width:], w_kv)
+
+    x, y, core = flip("dp", 1), flip("expert", 2), flip("expert", 1)
+    near, far = flip("context", 1), flip("context", 2)
+    greet([x, y, core] + [other("context", step) for step in range(1, contexts)])
+    back = GroupReturn(y_ref, *return_scratch, rows)
     back.start()
+
+    chunk = down_rows
+    chunks = (slice_rows + down_rows) // chunk
+    near_copies, far_copies, x_copies = [], [], []
+    for index in range(chunks):
+        span = pl.ds(index * chunk, chunk)
+        source = down_place(1) if index == chunks - 1 else gu_part_ref.at[1, span]
+        near_copies.append(
+            remote(source, near_in.at[span], near_sems.at[0, index], near_sems.at[1, index], near)
+        )
+        far_copies.append(
+            remote(
+                stage_a.at[span], far_in.at[span], far_sems.at[0, index], far_sems.at[1, index], far
+            )
+        )
 
     grad_part, gain_grad = norm_pull(residual_ref[...], ffn_gain_ref[...], dh2_ref[...])
     gains_ref[...] = jnp.zeros_like(gains_ref)
     gains_ref[1:2] = gain_grad
     dres[...] = c_ref[...].astype(F32) + grad_part
     dbranch[...] = dres[...].astype(BF)
+    for copy in stage_loads:
+        copy.wait()
+    for index in range(chunks):
+        span = pl.ds(index * chunk, chunk)
+        value = stage_a[span].astype(F32) + stage_b[span].astype(F32)
+        stage_a[span] = value.astype(BF)
+        if index == 0:
+            far_copies[0].start()
+    own_loads = [
+        load(6, gu_part_ref.at[0], stage_b.at[gu_span]),
+        load(7, down_place(0), stage_b.at[down_span]),
+    ]
     load_out.wait()
-    datt[...] = matmul(dbranch[...], w_out[...], NT).astype(BF)
+    datt[...] = matmul(dbranch[...], w_dense[...], NT).astype(BF)
+    load_w_q = load(8, w_qkv_ref.at[:, :query_width], w_dense)
     delta[...] = jnp.zeros_like(delta)
     for head in range(QUERY_HEADS):
         lanes = slice(head * HEAD_SIZE, (head + 1) * HEAD_SIZE)
-        turned_grad = datt[:, lanes].astype(F32).T
-        delta[head : head + 1] = jnp.sum(turned_grad * att_ref[head], axis=0, keepdims=True)
+        product = datt[:, lanes].astype(F32) * merged_ref[:, lanes].astype(F32)
+        delta[head : head + 1] = jnp.sum(product.T, axis=0, keepdims=True)
+
+    def dense_matmul(target, left, right):
+        for index in range(contexts):
+            lanes = slice(index * slice_rows, (index + 1) * slice_rows)
+            target[index] = matmul(left[:, lanes], right, TN).astype(BF)
+
+    middle = len(others) // 3
+    streams = []
+    for number, (part, target, lanes) in enumerate(
+        (
+            (dense, out_proj_ref, slice(0, D)),
+            (dense, qkv_grad_ref, slice(0, query_width)),
+            (dense_kv, qkv_grad_ref, slice(query_width, query_width + 2 * key_width)),
+        )
+    ):
+        scratch = others[number * middle : (number + 1) * middle]
+        streams.append(DenseReduce(part, *scratch[:-1], target, lanes, scratch[-1]))
+    out_proj, queries, keys_values = streams
+    dense_matmul(dense, merged_ref, dbranch[...])
+    out_proj.start()
+
     back.far()
 
     lax.fori_loop(0, me + 1, end_load, 0)
@@ -1319,16 +1497,20 @@
         return carry
 
     lax.fori_loop(0, me, earlier, 0)
+    for index in range(chunks):
+        near_copies[index].start()
+        if index > 0:
+            far_copies[index].start()
     pull(me)
-    back.middle()
-
+    out_proj.after_core()
+    out_proj.release()
     for head in range(QUERY_HEADS):
         lanes = slice(head * HEAD_SIZE, (head + 1) * HEAD_SIZE)
         dqkv[:, lanes] = unrotate(dq[head].T * scaling, cos_ref[...], sin_ref[...]).astype(BF)
-    for offset in range(0, query_width, 512):
-        lanes = slice(offset, offset + 512)
-        qkv_grad_ref[:, lanes] = matmul(h1_ref[...], dqkv[:, lanes], TN).astype(BF)
-        out_proj_ref[:, lanes] = matmul(merged_ref[...], dbranch[:, lanes], TN).astype(BF)
+    dense_matmul(dense, h1_ref, dqkv[:, :query_width])
+    queries.start()
+    back.middle()
+    queries.after_core()
 
     def later(step, carry):
         dkv_copy(step).wait_recv()
@@ -1343,26 +1525,100 @@
             dkv_sum[:, lanes] * scaling, cos_ref[...], sin_ref[...]
         ).astype(BF)
     dqkv[:, query_width + key_width :] = dkv_sum[:, key_width:].astype(BF)
-    qkv_grad_ref[:, query_width:] = matmul(h1_ref[...], dqkv[:, query_width:], TN).astype(BF)
-    load_qkv.wait()
-    grad_part, gain_grad = norm_pull(
-        x_ref[...].astype(F32), attn_gain_ref[...], matmul(dqkv[...], w_qkv[...], NT)
-    )
+    dense_matmul(dense_kv, h1_ref, dqkv[:, query_width:])
+    keys_values.start()
+    load_w_q.wait()
+    load_w_kv.wait()
+    dh1 = matmul(dqkv[:, :query_width], w_dense[...], NT)
+    dh1 = dh1 + matmul(dqkv[:, query_width:], w_kv[...], NT)
+    grad_part, gain_grad = norm_pull(x_ref[...].astype(F32), attn_gain_ref[...], dh1)
     gains_ref[0:1] = gain_grad
     packed_grad_ref[...] = dres[...] + grad_part
 
+    exchange = [core, y, x, near, far]
+    gain_copies = []
+
+    def gain_start():
+        step = len(gain_copies)
+        copy = remote(
+            gains_ref, gains_in.at[step], gain_sems.at[0, step], gain_sems.at[1, step], exchange[step]
+        )
+        copy.start()
+        gain_copies.append(copy)
+
+    def gain_add():
+        gain_copies[-1].wait()
+        gains_ref[...] += gains_in[len(gain_copies) - 1]
+
+    gain_start()
     back.settle()
     for index in range(2):
         span = slice(index * half, (index + 1) * half)
         packed_out_ref[span] = (residual_ref[span] + back.total(index)).astype(BF)
 
+    out_proj.after_y()
+    keys_values.after_core()
+    gain_add()
+    gain_start()
+    queries.after_y()
+    out_proj.after_x()
+    keys_values.after_y()
+    gain_add()
+    gain_start()
+    queries.after_x()
+    keys_values.after_x()
+    gain_add()
+    gain_start()
+
+    outs = []
+    for copy in own_loads:
+        copy.wait()
+
+    def weights_out(index):
+        near_copies[index].wait_recv()
+        far_copies[index].wait_recv()
+        span = pl.ds(index * chunk, chunk)
+        value = stage_b[span].astype(F32) + near_in[span].astype(F32)
+        stage_b[span] = (value + far_in[span].astype(F32)).astype(BF)
+        outs.append(load(9 + index, stage_b.at[span], weights_ref.at[dp, span]))
+        copy = remote(
+            stage_b.at[span],
+            weights_ref.at[dp, span],
+            x_sems.at[0, index],
+            x_sems.at[1, index],
+            x,
+        )
+        copy.start()
+        x_copies.append(copy)
+
+    weights_out(0)
+    out_proj.after_near_z()
+    queries.after_near_z()
+    keys_values.after_near_z()
+    gain_add()
+    gain_start()
+    out_proj.after_far_z()
+    queries.after_far_z()
+    keys_values.after_far_z()
+    gain_add()
+    weights_out(1)
+    for stream in streams:
+        stream.return_y()
+    weights_out(2)
+    for stream in streams:
+        stream.return_core()
+    for stream in streams:
+        stream.finish()
+
     def sent(step, carry):
         dkv_copy(step).wait_send()
         return carry
 
     lax.fori_loop(1, me + 1, sent, 0)
-    for send in sends:
-        send.wait()
+    for copy in near_copies + far_copies:
+        copy.wait_send()
+    for copy in x_copies + outs:
+        copy.wait()
 
 
 def attention_backward(
@@ -1370,7 +1626,6 @@
     residual,
     cotangent,
     merged,
-    att,
     logsum,
     query,
     h1,
@@ -1386,27 +1641,32 @@
     y,
     gu_part,
     down_part,
+    gu_far,
+    down_far,
 ):
     rows = x.shape[0]
     contexts = lax.axis_size("context")
+    query_width = QUERY_HEADS * HEAD_SIZE
     kv_width = 2 * KEY_VALUE_HEADS * HEAD_SIZE
+    slice_rows, down_rows = gu_far.shape[0], down_far.shape[0]
+    total = slice_rows + down_rows
     shape = jax.ShapeDtypeStruct
+    dma = pltpu.SemaphoreType.DMA
     return pl.pallas_call(
         backward_kernel,
         out_shape=[
             shape((rows, D), BF),
             shape((rows, D), F32),
             shape((8, D), F32),
-            shape(w_out.shape, BF),
-            shape(w_qkv.shape, BF),
-            shape(gu_part.shape[1:], BF),
-            shape((down_part.shape[1] // 2, D), BF),
+            shape((slice_rows, D), BF),
+            shape((slice_rows, query_width + kv_width), BF),
+            shape((2, total, D), BF),
         ],
-        in_specs=[VM] * 14 + [ANY] * 6,
-        out_specs=[VM] * 5 + [ANY] * 2,
+        in_specs=[VM] * 13 + [ANY] * 8,
+        out_specs=[VM] * 5 + [ANY],
         scratch_shapes=[
-            pltpu.VMEM(w_qkv.shape, BF),
             pltpu.VMEM(w_out.shape, BF),
+            pltpu.VMEM((D, kv_width), BF),
             pltpu.VMEM(kv.shape, BF),
             pltpu.VMEM((rows, D), F32),
             pltpu.VMEM((rows, D), BF),
@@ -1417,15 +1677,28 @@
             pltpu.VMEM((rows, kv_width), F32),
             pltpu.VMEM((contexts, rows, kv_width), BF),
             pltpu.VMEM((contexts, rows, kv_width), BF),
-            pltpu.VMEM((rows, w_qkv.shape[1]), BF),
-            pltpu.SemaphoreType.DMA((2,)),
-            pltpu.SemaphoreType.DMA((contexts,)),
-            pltpu.SemaphoreType.DMA((2, 2)),
-            pltpu.SemaphoreType.DMA((2, contexts)),
+            pltpu.VMEM((rows, query_width + kv_width), BF),
+            pltpu.VMEM((contexts, slice_rows, D), BF),
+            pltpu.VMEM((contexts, slice_rows, kv_width), BF),
+            pltpu.VMEM((total, D), BF),
+            pltpu.VMEM((total, D), BF),
+            pltpu.VMEM((total, D), BF),
+            pltpu.VMEM((total, D), BF),
+            pltpu.VMEM((5, 8, D), F32),
+            dma((9 + total // down_rows,)),
+            dma((contexts,)),
+            dma((2, contexts)),
+            dma((2, total // down_rows)),
+            dma((2, total // down_rows)),
+            dma((2, total // down_rows)),
+            dma((2, 5)),
         ]
-        + GroupReturn.scratch(rows),
+        + GroupReturn.scratch(rows)
+        + DenseReduce.scratch(contexts, slice_rows, D)
+        + DenseReduce.scratch(contexts, slice_rows, query_width)
+        + DenseReduce.scratch(contexts, slice_rows, kv_width),
         compiler_params=pltpu.CompilerParams(
-            collective_id=3, has_side_effects=True, vmem_limit_bytes=60 << 20
+            collective_id=3, has_side_effects=True, vmem_limit_bytes=62 << 20
         ),
         cost_estimate=pl.CostEstimate(
             flops=2 * rows * D * 8000, bytes_accessed=40 << 20, transcendentals=rows * rows * 48
@@ -1435,7 +1708,6 @@
         residual,
         cotangent,
         merged,
-        att,
         logsum,
         query,
         h1,
@@ -1451,357 +1723,9 @@
         y,
         gu_part,
         down_part,
-    )
-
-
-def bit_of(axis, bit):
-    return lax.rem(lax.axis_index(axis) // bit, 2)
-
-
-class DenseReduce:
-    def __init__(self, part, keep, near, first, second, third, fourth, out, sems):
-        self.part, self.keep, self.near, self.first = part, keep, near, first
-        self.second, self.third, self.fourth, self.out = second, third, fourth, out
-        self.sems = sems
-        self.count = 0
-        self.width = part.shape[2] // 2
-        self.rows = part.shape[1] // 8
-        self.x, self.y, self.core = flip("dp", 1), flip("expert", 2), flip("expert", 1)
-        self.xb, self.yb, self.cb = bit_of("dp", 1), bit_of("expert", 2), bit_of("expert", 1)
-        self.flows = (
-            (self.y, self.yb, self.x, self.xb),
-            (self.x, self.xb, self.y, self.yb),
-        )
-        self.pending = []
-
-    def link(self, src, dst, peer):
-        number = self.count
-        self.count += 1
-        copy = remote(src, dst, self.sems.at[0, number], self.sems.at[1, number], peer)
-        copy.start()
-        self.pending.append(copy)
-        return copy
-
-    def lanes(self, flow):
-        return slice(flow * self.width, (flow + 1) * self.width)
-
-    def span(self, bit, size, base=0):
-        return pl.ds(pl.multiple_of(base + bit * size, 16), size)
-
-    def start(self):
-        size = 4 * self.rows
-        self.load = pltpu.make_async_copy(
-            self.part.at[:, self.span(self.cb, size)], self.keep, self.sems.at[0, 16]
-        )
-        self.load.start()
-        self.copies = [
-            self.link(self.part.at[:, self.span(1 - self.cb, size)], self.near, self.core)
-        ]
-
-    def after_core(self):
-        self.load.wait()
-        self.copies[0].wait_recv()
-        slices = self.part.shape[0]
-        for index in range(slices):
-            value = self.near[index].astype(F32) + self.keep[index].astype(F32)
-            self.near[index] = value.astype(BF)
-        size = 2 * self.rows
-        self.copies = [
-            self.link(
-                self.near.at[:, self.span(1 - bit, size), self.lanes(flow)],
-                self.first.at[flow],
-                peer,
-            )
-            for flow, (peer, bit, _, _) in enumerate(self.flows)
-        ]
-
-    def after_first(self):
-        size = 2 * self.rows
-        copies = []
-        for flow, (_, bit, peer, later_bit) in enumerate(self.flows):
-            self.copies[flow].wait_recv()
-            for index in range(self.part.shape[0]):
-                value = self.near[index, self.span(bit, size), self.lanes(flow)].astype(F32)
-                value = value + self.first[flow, index].astype(F32)
-                self.first[flow, index] = value.astype(BF)
-            copies.append(
-                self.link(
-                    self.first.at[flow, :, self.span(1 - later_bit, self.rows)],
-                    self.second.at[flow],
-                    peer,
-                )
-            )
-        self.copies = copies
-
-    def after_second(self):
-        peer, bit = flip("context", 1), bit_of("context", 1)
-        copies = []
-        for flow, (_, _, _, later_bit) in enumerate(self.flows):
-            self.copies[flow].wait_recv()
-            for index in range(self.part.shape[0]):
-                value = self.first[flow, index, self.span(later_bit, self.rows)].astype(F32)
-                place = (flow, index)
-                self.second[place] = (value + self.second[place].astype(F32)).astype(BF)
-            for high in range(2):
-                copies.append(
-                    self.link(
-                        self.second.at[flow, 2 * high + 1 - bit],
-                        self.third.at[flow, high],
-                        peer,
-                    )
-                )
-        self.copies = copies
-
-    def after_third(self):
-        bit = bit_of("context", 1)
-        peer, later_bit = flip("context", 2), bit_of("context", 2)
-        copies = []
-        for flow in range(2):
-            for high in range(2):
-                self.copies[2 * flow + high].wait_recv()
-                value = self.second[flow, 2 * high + bit].astype(F32)
-                value = value + self.third[flow, high].astype(F32)
-                self.third[flow, high] = value.astype(BF)
-            copies.append(
-                self.link(self.third.at[flow, 1 - later_bit], self.fourth.at[flow], peer)
-            )
-        self.copies = copies
-
-    def place(self, flow, cuts):
-        _, bit, _, later_bit = self.flows[flow]
-        base = self.cb * 4 * self.rows + bit * 2 * self.rows
-        if cuts:
-            return pl.ds(pl.multiple_of(base, 16), 2 * self.rows)
-        return pl.ds(pl.multiple_of(base + later_bit * self.rows, 16), self.rows)
-
-    def after_fourth(self):
-        bit = bit_of("context", 2)
-        copies = []
-        for flow, (_, _, peer, _) in enumerate(self.flows):
-            self.copies[flow].wait_recv()
-            value = self.third[flow, bit].astype(F32) + self.fourth[flow].astype(F32)
-            rows, lanes = self.place(flow, 0), self.lanes(flow)
-            self.out[rows, lanes] = value.astype(BF)
-            copies.append(self.link(self.out.at[rows, lanes], self.out.at[rows, lanes], peer))
-        self.copies = copies
-
-    def spread(self):
-        copies = []
-        for flow, (peer, _, _, _) in enumerate(self.flows):
-            self.copies[flow].wait_recv()
-            rows, lanes = self.place(flow, 1), self.lanes(flow)
-            copies.append(self.link(self.out.at[rows, lanes], self.out.at[rows, lanes], peer))
-        self.copies = copies
-
-    def last(self):
-        for copy in self.copies:
-            copy.wait_recv()
-        rows = self.span(self.cb, 4 * self.rows)
-        self.copies = [self.link(self.out.at[rows], self.out.at[rows], self.core)]
-
-    def finish(self):
-        self.copies[0].wait_recv()
-        for copy in self.pending:
-            copy.wait_send()
-
-    @staticmethod
-    def scratch(contexts, rows, width):
-        quarter = rows // 8
-        return [
-            pltpu.VMEM((contexts, 4 * quarter, width), BF),
-            pltpu.VMEM((contexts, 4 * quarter, width), BF),
-            pltpu.VMEM((2, contexts, 2 * quarter, width // 2), BF),
-            pltpu.VMEM((2, contexts, quarter, width // 2), BF),
-            pltpu.VMEM((2, contexts // 2, quarter, width // 2), BF),
-            pltpu.VMEM((2, quarter, width // 2), BF),
-            pltpu.SemaphoreType.DMA((2, 17)),
-        ]
-
-
-def finish_kernel(
-    gains_ref,
-    gu_part_ref,
-    down_part_ref,
-    gu_far_ref,
-    down_far_ref,
-    gu_near_ref,
-    down_near_ref,
-    out_proj_ref,
-    qkv_grad_ref,
-    gains_out_ref,
-    out_proj_out_ref,
-    qkv_grad_out_ref,
-    weights_out_ref,
-    part,
-    arrived,
-    passed,
-    gains_in,
-    load_sems,
-    z_sems,
-    x_sems,
-    gain_sems,
-    *dense_scratch,
-):
-    slice_rows = gu_far_ref.shape[0]
-    down_rows = down_far_ref.shape[0]
-    dp = lax.axis_index("dp")
-    x, z_far = flip("dp", 1), flip("context", 2)
-
-    def down_place(code):
-        return pl.ds(
-            pl.multiple_of(lax.rem(turned("context", code), 2) * down_rows, 16), down_rows
-        )
-
-    gu_span, down_span = pl.ds(0, slice_rows), pl.ds(slice_rows, down_rows)
-    loads = []
-    for index, (code, gu_in, down_in) in enumerate(
-        ((2, gu_far_ref, down_far_ref), (0, gu_near_ref, down_near_ref))
-    ):
-        for number, (src, dst) in enumerate(
-            (
-                (gu_part_ref.at[code], part.at[index, gu_span]),
-                (down_part_ref.at[code // 2, down_place(code)], part.at[index, down_span]),
-                (gu_in, arrived.at[index, gu_span]),
-                (down_in, arrived.at[index, down_span]),
-            )
-        ):
-            loads.append(pltpu.make_async_copy(src, dst, load_sems.at[4 * index + number]))
-    for load in loads:
-        load.start()
-
-    exchange = [
-        flip("expert", 1),
-        flip("expert", 2),
-        flip("dp", 1),
-        flip("context", 1),
-        flip("context", 2),
-    ]
-    greet(exchange)
-
-    middle = len(dense_scratch) // 2
-    qkv_scratch, out_scratch = dense_scratch[:middle], dense_scratch[middle:]
-    qkv = DenseReduce(qkv_grad_ref, *qkv_scratch[:-1], qkv_grad_out_ref, qkv_scratch[-1])
-    out = DenseReduce(out_proj_ref, *out_scratch[:-1], out_proj_out_ref, out_scratch[-1])
-    dense = (out, qkv)
-    for array in dense:
-        array.start()
-
-    gains_out_ref[...] = gains_ref[...]
-    gain_copies = []
-
-    def gain_start(step):
-        copy = remote(
-            gains_out_ref,
-            gains_in.at[step],
-            gain_sems.at[0, step],
-            gain_sems.at[1, step],
-            exchange[step],
-        )
-        copy.start()
-        gain_copies.append(copy)
-
-    def gain_add(step):
-        gain_copies[step].wait()
-        gains_out_ref[...] += gains_in[step]
-
-    gain_start(0)
-    for load in loads:
-        load.wait()
-    chunk = down_rows
-    chunks = (slice_rows + down_rows) // chunk
-    z_copies, x_copies = [], []
-    for index in range(chunks):
-        span = pl.ds(index * chunk, chunk)
-        value = part[0, span].astype(F32) + arrived[0, span].astype(F32)
-        part[0, span] = value.astype(BF)
-        copy = remote(
-            part.at[0, span], passed.at[span], z_sems.at[0, index], z_sems.at[1, index], z_far
-        )
-        copy.start()
-        z_copies.append(copy)
-
-    def experts_out(index):
-        z_copies[index].wait_recv()
-        span = pl.ds(index * chunk, chunk)
-        value = part[1, span].astype(F32) + arrived[1, span].astype(F32)
-        weights_out_ref[dp, span] = (value + passed[span].astype(F32)).astype(BF)
-        copy = remote(
-            weights_out_ref.at[dp, span],
-            weights_out_ref.at[dp, span],
-            x_sems.at[0, index],
-            x_sems.at[1, index],
-            x,
-        )
-        copy.start()
-        x_copies.append(copy)
-
-    gain_add(0)
-    gain_start(1)
-    for array in dense:
-        array.after_core()
-    gain_add(1)
-    gain_start(2)
-    for array in dense:
-        array.after_first()
-    gain_add(2)
-    gain_start(3)
-    for index in range(chunks):
-        experts_out(index)
-    gain_add(3)
-    gain_start(4)
-    for array in dense:
-        array.after_second()
-    gain_add(4)
-    for array in dense:
-        array.after_third()
-    for array in dense:
-        array.after_fourth()
-    for array in dense:
-        array.spread()
-    for array in dense:
-        array.last()
-    for array in dense:
-        array.finish()
-    for copy in z_copies:
-        copy.wait_send()
-    for copy in x_copies:
-        copy.wait()
-
-
-def finish(gains, gu_part, down_part, gu_far, down_far, gu_near, down_near, out_proj, qkv_grad):
-    contexts = lax.axis_size("context")
-    slice_rows, down_rows = gu_far.shape[0], down_far.shape[0]
-    total = slice_rows + down_rows
-    shape = jax.ShapeDtypeStruct
-    out_proj = out_proj.reshape(contexts, slice_rows, -1)
-    qkv_grad = qkv_grad.reshape(contexts, slice_rows, -1)
-    return pl.pallas_call(
-        finish_kernel,
-        out_shape=[
-            shape(gains.shape, F32),
-            shape(out_proj.shape[1:], BF),
-            shape(qkv_grad.shape[1:], BF),
-            shape((2, total, D), BF),
-        ],
-        in_specs=[VM] + [ANY] * 8,
-        out_specs=[VM] * 4,
-        scratch_shapes=[
-            pltpu.VMEM((2, total, D), BF),
-            pltpu.VMEM((2, total, D), BF),
-            pltpu.VMEM((total, D), BF),
-            pltpu.VMEM((5,) + gains.shape, F32),
-            pltpu.SemaphoreType.DMA((8,)),
-            pltpu.SemaphoreType.DMA((2, total // down_rows)),
-            pltpu.SemaphoreType.DMA((2, total // down_rows)),
-            pltpu.SemaphoreType.DMA((2, 5)),
-        ]
-        + DenseReduce.scratch(contexts, slice_rows, qkv_grad.shape[2])
-        + DenseReduce.scratch(contexts, slice_rows, out_proj.shape[2]),
-        compiler_params=pltpu.CompilerParams(
-            collective_id=4, has_side_effects=True, vmem_limit_bytes=60 << 20
-        ),
-        cost_estimate=pl.CostEstimate(flops=0, bytes_accessed=40 << 20, transcendentals=0),
-    )(gains, gu_part, down_part, gu_far, down_far, gu_near, down_near, out_proj, qkv_grad)
+        gu_far,
+        down_far,
+    )
 
 
 def fast_body(
@@ -1823,19 +1747,18 @@
     expert_total = expert_gate_up.shape[0] * lax.axis_size("expert")
     attn_gain, ffn_gain = attn_gain[None], ffn_gain[None]
     begins, cosine, sine, share = prepare(routes, gates, doc_starts, rows, expert_total)
-    (h1, query, att, logsum, merged, residual, h2, kv, c_all, share_all) = attention_forward(
+    h1, query, logsum, merged, residual, h2, kv, c_all, share_all = attention_forward(
         x, share, begins, cosine, sine, attn_gain, ffn_gain, c, w_qkv, w_out
     )
     h2_all, dgu, hidden, du = experts(h2, share_all, c_all, expert_gate_up, expert_down)
     dh2, gu_part, down_part, gu_far, down_far, y = expert_weights(
         h2_all, dgu, hidden, c_all, du, expert_down
     )
-    packed_out, packed_grad, gains, out_proj, qkv_grad, gu_near, down_near = attention_backward(
+    packed_out, packed_grad, gains, out_proj, qkv_grad, weights = attention_backward(
         dh2,
         residual,
         c,
         merged,
-        att,
         logsum,
         query,
         h1,
@@ -1851,9 +1774,8 @@
         y,
         gu_part,
         down_part,
-    )
-    gains, out_proj, qkv_grad, weights = finish(
-        gains, gu_part, down_part, gu_far, down_far, gu_near, down_near, out_proj, qkv_grad
+        gu_far,
+        down_far,
     )
     slice_rows = D // contexts
     gains = lax.dynamic_slice_in_dim(gains, lax.axis_index("context") * slice_rows, slice_rows, 1)

time: 375 us -> 348 us (0.928)
  the two profiles are of different devices: /device:TPU:27 before, /device:TPU:0 now
where the time goes in v3:
time: 348 us; the launch traced here: 341 us
  Pallas kernels  319 us (92%)
  other arithmetic  14.8 us (4%)
  local copies, waits for them, and re-layouts  6.08 us (2%)
    pallas_call x1, Pallas kernels, attention_backward(): pl.pallas_call(backward_kernel, out_shape=[shape((rows, D), BF), shape((r...  176 us
    pallas_call x1, Pallas kernels, experts(): pl.pallas_call(experts_kernel, out_shape=[shape((total, D), BF), shape((t...  54.8 us
    pallas_call x1, Pallas kernels, expert_weights(): pl.pallas_call(weights_kernel, out_shape=[shape((rows, D), F32), shape(gu...  48.7 us
    pallas_call x1, Pallas kernels, attention_forward(): pl.pallas_call(attention_kernel, out_shape=[shape((rows, D), BF), shape((...  39.4 us

profile of v3, /device:TPU:0, one launch (start us, length us, event | category | flops | bytes accessed | tf_op | source)
XLA Modules:
  0.0 341.2 jit_solution(11922625642639709184)
XLA Ops:
  0.6 0.7 select_reduce_fusion.1
  1.4 0.0 copy-start.4
  1.4 0.5 fusion
  2.0 0.8 pad_maximum_fusion
  2.8 1.3 broadcast_in_dim.48.attn_gain_ref
  4.1 1.3 broadcast_in_dim.49.ffn_gain_ref
  5.4 1.3 select_reduce_fusion.share_ref
  6.7 0.0 copy-done.4
  6.7 39.4 %shard_map.170 = (bf16[256,1536]{1,0:T(8,128)(2,1)}, bf16[12,256,128]{2,1,0:T(8,128)(2,1)}, f32[16,256]{1,0:T(8,128)}, bf16[256,1536]{1,0:T(8,128)(2,1)}, f32[25...) custom-call(bf16[256,1536]{1,0:T(8,128)(2,1)} %bitcast.8, ...), custom_call_target="tpu_custom_call" | custom-call | flops 3221225472 | bytes 31457280 | tf_op jit(solution)/shard_map/pallas_call | solution.py:722
  46.1 54.8 %shard_map.171 = (bf16[2048,1536]{1,0:T(8,128)(2,1)}, bf16[2048,1536]{1,0:T(8,128)(2,1)}, bf16[2048,768]{1,0:T(8,128)(2,1)}, bf16[2048,1536]{1,0:T(8,128)(2,1)}) custom-call(bf16[256,1536]{1,0:T(8,128)(2,1)} %get-tuple-element.33.h2_ref, f32[8,8,256]{2,1,0:T(8,128)} %get-tuple-element.34.share_ref, bf16[2048,1536]{1,0:T(8,128)(2,1)} %get-tuple-element.35.c_all_ref, ...), custom_call_target="tpu_custom_call" | custom-call | flops 24159191040 | bytes 52428800 | tf_op jit(solution)/shard_map/pallas_call | solution.py:885
  100.9 48.7 %shard_map.172 = (f32[256,1536]{1,0:T(8,128)}, bf16[4,384,1536]{2,1,0:T(8,128)(2,1)}, bf16[2,384,1536]{2,1,0:T(8,128)(2,1)}, bf16[384,1536]{1,0:T(8,128)(2,1)}, ...) custom-call(bf16[2048,1536]{1,0:T(8,128)(2,1)} %get-tuple-element.36.h2_all_ref, ...), custom_call_target="tpu_custom_call" | custom-call | flops 19327352832 | bytes 52428800 | tf_op jit(solution)/shard_map/pallas_call | solution.py:1125
  149.6 176.3 %shard_map.173 = (bf16[256,1536]{1,0:T(8,128)(2,1)}, f32[256,1536]{1,0:T(8,128)}, f32[8,1536]{1,0:T(8,128)}, bf16[384,1536]{1,0:T(8,128)(2,1)}, bf16[384,2048]{1...) custom-call(f32[256,1536]{1,0:T(8,128)} %get-tuple-element.40.dh2_ref, f32[256,1536]{1,0:T(8,128)} %get-tuple-element.41.residual_ref, ...), custom_call_target="tpu_custom_call" | custom-call | flops 6291456000 | bytes 41943040 | tf_op jit(solution)/shard_map/pallas_call | solution.py:1655
  325.9 0.0 copy-start.1
  325.9 4.6 %slice_convert_fusion = f32[2,384,1536]{2,1,0:T(8,128)} fusion(bf16[2,576,1536]{2,1,0:T(8,128)(2,1)} %get-tuple-element.57), kind=kLoop, calls=%fused_computation | loop fusion | flops 1179648 | bytes 7077888 | tf_op jit(solution)/shard_map/convert_element_type | solution.py:1789
  330.5 0.0 copy-start.2
  330.5 0.0 copy-done.1
  330.5 2.0 convert_element_type.20
  332.6 0.0 copy-done.2
  332.6 0.0 copy-start.3
  332.6 0.0 copy-start
  332.6 1.7 convert_element_type.21
  334.3 3.0 slice_convert_fusion.1
  337.2 1.4 dynamic-slice_reduce_fusion
  338.7 0.0 copy-done.3
  338.7 0.9 copy.23
  339.6 0.0 copy-done
  339.6 1.1 copy.24
  (3 shorter events, 0.0 us)
Async XLA Ops:
  1.4 5.3 %copy-start.4 = (s32[256]{0:T(256)}, s32[256]{0:T(256)S(1)}, u32[]{:S(2)}) copy-start(s32[256]{0:T(256)S(1)} %select_reduce_fusion.1) | copy-start | bytes 3076
  325.9 4.6 %copy-start.1 = (bf16[384,2048]{1,0:T(8,128)(2,1)S(1)}, bf16[384,2048]{1,0:T(8,128)(2,1)}, u32[]{:S(2)}) copy-start(bf16[384,2048]{1,0:T(8,128)(2,1)} %get-tuple-element.55) | copy-start | bytes 4718596
  330.5 2.0 copy-start.2
  332.6 6.1 %copy-start.3 = (bf16[256,1536]{1,0:T(8,128)(2,1)S(1)}, bf16[256,1536]{1,0:T(8,128)(2,1)}, u32[]{:S(2)}) copy-start(bf16[256,1536]{1,0:T(8,128)(2,1)} %get-tuple-element.52) | copy-start | bytes 2359300
  332.6 7.0 %copy-start = (f32[256,1536]{1,0:T(8,128)S(1)}, f32[256,1536]{1,0:T(8,128)}, u32[]{:S(2)}) copy-start(f32[256,1536]{1,0:T(8,128)} %get-tuple-element.53) | copy-start | bytes 4718596
